TPU v7x, 768 devices: a whole 4x8x12 slice. The times are simulated.
768 devices in a mesh: wide: 96 (over y, z), narrow: 8 (over x, core).
Axes of the slice: x: 4, y: 8, z: 12, core: 2. Of those that a mesh axis runs over, the one named last changes fastest.
Arguments:
- velocity: float32 [3, 768, 128, 128], P(None, 'wide', 'narrow'), may hold values from -6 to 6
- reaction: float32 [768, 128, 128], P('wide', 'narrow'), may hold values from 1 to 64
Outputs:
- advection: float32 [3, 768, 128, 128], P(None, 'wide', 'narrow')
- pressure: float32 [768, 128, 128], P('wide', 'narrow')
- residual: float32 [768, 128, 128], P('wide', 'narrow')
All inputs are finite; a program needn't handle non-finite values.
Results may differ from a plain program's by a relative error of at most 0.00028.
Values sent between devices are 32-bit elements; how exact they have to be, the bound alone decides.
A program may use at most 32 MiB of HBM per device.

v0:
```python
import jax
import jax.numpy as jnp
import numpy as np
from jax import lax
from jax.sharding import PartitionSpec as P

ITERS = 3


def padded_2(block, sides, width):
    for axis, dim in sides:
        count = lax.axis_size(axis)
        forward = [(i, i + 1) for i in range(count - 1)]
        backward = [(target, source) for source, target in forward]
        low = lax.ppermute(
            lax.slice_in_dim(block, block.shape[dim] - width, None, axis=dim), axis, forward
        )
        high = lax.ppermute(lax.slice_in_dim(block, 0, width, axis=dim), axis, backward)
        block = jnp.concatenate([low, block, high], axis=dim)
    return block


def legendre_pair(order, nodes):
    p_prev = np.ones(nodes.shape)
    p_now = nodes * 1.0
    for k in range(2, order + 1):
        p_next = ((2 * k - 1) * nodes * p_now - (k - 1) * p_prev) / k
        p_prev = p_now
        p_now = p_next
    return (p_now, p_prev)


def spectral_tables():
    degree = 7
    points = degree + 1
    gll_nodes = np.cos(np.pi * np.arange(points) / degree)
    for sweep in range(100):
        p_now, p_prev = legendre_pair(degree, gll_nodes)
        gll_nodes = gll_nodes - (gll_nodes * p_now - p_prev) / ((degree + 1) * p_now)
    gll_nodes = np.sort(gll_nodes)
    legendre_vals, unused_prev = legendre_pair(degree, gll_nodes)
    gll_weights = 2.0 / (degree * (degree + 1) * legendre_vals**2)
    derivative = np.zeros((points, points))
    for row_index in range(points):
        for col_index in range(points):
            if row_index != col_index:
                derivative[row_index, col_index] = legendre_vals[row_index] / (
                    legendre_vals[col_index] * (gll_nodes[row_index] - gll_nodes[col_index])
                )
    derivative[0, 0] = -degree * (degree + 1) / 4.0
    derivative[-1, -1] = degree * (degree + 1) / 4.0
    gauss_nodes = np.cos(np.pi * (np.arange(12) + 0.75) / 12.5)
    for sweep in range(100):
        p_now, p_prev = legendre_pair(12, gauss_nodes)
        slope = 12 * (gauss_nodes * p_now - p_prev) / (gauss_nodes * gauss_nodes - 1.0)
        gauss_nodes = gauss_nodes - p_now / slope
    gauss_nodes = np.sort(gauss_nodes)
    p_now, p_prev = legendre_pair(12, gauss_nodes)
    slope = 12 * (gauss_nodes * p_now - p_prev) / (gauss_nodes * gauss_nodes - 1.0)
    gauss_weights = 2.0 / ((1.0 - gauss_nodes**2) * slope**2)
    interpolate = np.ones((12, points))
    for col_index in range(points):
        for other in range(points):
            if other != col_index:
                interpolate[:, col_index] *= (gauss_nodes - gll_nodes[other]) / (
                    gll_nodes[col_index] - gll_nodes[other]
                )
    return (gll_weights, derivative, gauss_weights, interpolate)


def along_axis(values, matrix, axis_pos):
    highest = lax.Precision.HIGHEST
    shape = values.shape
    inner_len = matrix.shape[1]
    blocks = shape[axis_pos] // inner_len
    split = values.reshape(shape[:axis_pos] + (blocks, inner_len) + shape[axis_pos + 1 :])
    letters = ["a", "b", "c", "d"]
    in_names = list(letters)
    out_names = list(letters)
    in_names[axis_pos] = "ek"
    out_names[axis_pos] = "ep"
    form = "".join(in_names) + ",pk->" + "".join(out_names)
    result = jnp.einsum(form, split, matrix, precision=highest)
    return result.reshape(shape[:axis_pos] + (blocks * matrix.shape[0],) + shape[axis_pos + 1 :])


def pair_sum(padded, axis_pos, length):
    self_vals = lax.slice_in_dim(padded, 1, length + 1, axis=axis_pos)
    left_vals = lax.slice_in_dim(padded, 0, length, axis=axis_pos)
    right_vals = lax.slice_in_dim(padded, 2, length + 2, axis=axis_pos)
    dims_shape = [1, 1, 1, 1]
    dims_shape[axis_pos] = length
    position = jnp.arange(length).reshape(dims_shape) % 8
    return (
        self_vals
        + jnp.where(position == 0, left_vals, 0.0)
        + jnp.where(position == 7, right_vals, 0.0)
    )


def gather_scatter(values):
    width_x, width_y, width_z = (values.shape[1], values.shape[2], values.shape[3])
    padded = padded_2(values, (("wide", 1),), 1)
    summed = pair_sum(padded, 1, width_x)
    padded = padded_2(summed, (("narrow", 2),), 1)
    summed = pair_sum(padded, 2, width_y)
    padded = jnp.pad(summed, ((0, 0), (0, 0), (0, 0), (1, 1)))
    return pair_sum(padded, 3, width_z)


def edge_factor(position, total):
    local_pos = position % 8
    shared = (local_pos == 0) & (position > 0) | (local_pos == 7) & (position < total - 1)
    return jnp.where(shared, 0.5, 1.0).astype(jnp.float32)


def merged_dots(first, second, inverse_mult):
    return lax.psum(
        (jnp.sum(first * first * inverse_mult), jnp.sum(second * first * inverse_mult)),
        ("wide", "narrow"),
    )


def per_device(velocity, reaction):
    gll_weights, derivative, gauss_weights, interpolate = spectral_tables()
    width_x, width_y, width_z = reaction.shape
    blocks_x, blocks_y, blocks_z = (width_x // 8, width_y // 8, width_z // 8)
    interp = jnp.asarray(interpolate, dtype=jnp.float32)
    interp_back = jnp.asarray(interpolate.T, dtype=jnp.float32)
    gradint = jnp.asarray(interpolate @ derivative, dtype=jnp.float32)
    deriv = jnp.asarray(derivative, dtype=jnp.float32)
    deriv_back = jnp.asarray(derivative.T, dtype=jnp.float32)
    mass_local = jnp.asarray(
        np.tile(gll_weights, blocks_x)[:, None, None]
        * np.tile(gll_weights, blocks_y)[None, :, None]
        * np.tile(gll_weights, blocks_z)[None, None, :],
        dtype=jnp.float32,
    )[None]
    gauss_x = jnp.asarray(np.tile(gauss_weights, blocks_x), dtype=jnp.float32)
    gauss_y = jnp.asarray(np.tile(gauss_weights, blocks_y), dtype=jnp.float32)
    gauss_z = jnp.asarray(np.tile(gauss_weights, blocks_z), dtype=jnp.float32)
    start_x = lax.axis_index("wide") * width_x + jnp.arange(width_x)
    start_y = lax.axis_index("narrow") * width_y + jnp.arange(width_y)
    factor_x = edge_factor(start_x, width_x * lax.axis_size("wide"))
    factor_y = edge_factor(start_y, width_y * lax.axis_size("narrow"))
    factor_z = edge_factor(jnp.arange(width_z), width_z)
    inverse_mult = (factor_x[:, None, None] * factor_y[None, :, None] * factor_z[None, None, :])[
        None
    ]
    vel_z = along_axis(velocity, interp, 3)
    grad_z = along_axis(velocity, gradint, 3)
    vel_zy = along_axis(vel_z, interp, 2)
    vel_zgy = along_axis(vel_z, gradint, 2)
    grad_zy = along_axis(grad_z, interp, 2)
    fine_vel = along_axis(vel_zy, interp, 1)
    product = fine_vel[0:1] * along_axis(vel_zy, gradint, 1)
    product = product + fine_vel[1:2] * along_axis(vel_zgy, interp, 1)
    product = product + fine_vel[2:3] * along_axis(grad_zy, interp, 1)
    weighted = (
        product * (gauss_x[:, None, None] * gauss_y[None, :, None] * gauss_z[None, None, :])[None]
    )
    weak_conv = along_axis(
        along_axis(along_axis(weighted, interp_back, 1), interp_back, 2), interp_back, 3
    )
    advection = gather_scatter(weak_conv) / (mass_local / inverse_mult)
    forward = velocity - 0.05 * advection
    divergence = (
        along_axis(forward[0:1], deriv, 1)
        + along_axis(forward[1:2], deriv, 2)
        + along_axis(forward[2:3], deriv, 3)
    )
    rhs = -gather_scatter(mass_local * divergence)
    react_mass = mass_local * reaction[None]
    pressure = jnp.zeros_like(rhs)
    residual = rhs
    direction = rhs
    along_dir = rhs
    gamma_old = None
    step_old = None
    for iteration in range(ITERS):
        local_sum = along_axis(mass_local * along_axis(residual, deriv, 1), deriv_back, 1)
        local_sum = local_sum + along_axis(
            mass_local * along_axis(residual, deriv, 2), deriv_back, 2
        )
        local_sum = local_sum + along_axis(
            mass_local * along_axis(residual, deriv, 3), deriv_back, 3
        )
        image_dir = gather_scatter(local_sum + react_mass * residual)
        gamma_new, curvature = merged_dots(residual, image_dir, inverse_mult)
        if iteration == 0:
            step_size = gamma_new / curvature
            direction = residual
            along_dir = image_dir
        else:
            ratio_now = gamma_new / gamma_old
            step_size = gamma_new / (curvature - ratio_now * gamma_new / step_old)
            direction = residual + ratio_now * direction
            along_dir = image_dir + ratio_now * along_dir
        pressure = pressure + step_size * direction
        residual = residual - step_size * along_dir
        gamma_old = gamma_new
        step_old = step_size
    return (advection, pressure[0], residual[0])


def solution(mesh):
    return jax.shard_map(
        per_device,
        mesh=mesh,
        in_specs=(P(None, "wide", "narrow", None), P("wide", "narrow", None)),
        out_specs=(
            P(None, "wide", "narrow", None),
            P("wide", "narrow", None),
            P("wide", "narrow", None),
        ),
        check_vma=False,
    )
```

profile of v0, /device:TPU:1, one launch (start us, length us, event | category | flops | bytes accessed | tf_op | source)
XLA Modules:
  0.0 504.1 jit_solution(5650991814764494032)
XLA Ops:
  0.6 1.4 copy.39
  2.7 4.3 convolution_bitcast_fusion
  7.0 4.3 convolution_bitcast_fusion.1
  11.4 3.8 copy.41
  15.1 1.5 reshape_reshape.8
  16.7 1.7 convolution_bitcast_fusion.8
  18.4 1.7 convolution_bitcast_fusion.7
  20.1 3.9 copy.45
  24.1 1.5 reshape_reshape.18
  35.2 1.8 reshape_reshape.20
  37.0 23.4 %fusion.2 = f32[3,8,16,128]{2,3,1,0:T(8,128)} fusion(f32[8,12,1,1,1]{1,0,4,3,2:T(8,128)S(1)} %copy-done.13, f32[3,8,16,16,12]{4,3,2,1,0:T(8,128)S(1)} %reshape_reshape.20), kind=kOutput, calls=%fused_computation.4 | convolution fusion | flops 7077888 | bytes 491904 | tf_op jit(solution)/shard_map/abcek,pk->abcep/dot_general | solution.py:83
  60.4 1.9 copy.51
  62.6 1.3 collective-permute-start.1
  63.9 5.5 %collective-permute-start = (f32[3,1,16,128]{3,1,2,0:T(1,128)S(1)}, f32[3,1,16,128]{3,1,2,0:T(1,128)S(1)}, u32[]{:S(2)}, u32[]{:S(2)}) collective-permute-start(f32[3,1,16,128]{3,1,2,0:T(1,128)S(1)} %get-tuple-element.35), channel_id=1, source_target_pairs={{0,8},{8,16},{16,24},{24,32},{32,40},{40,48},{48,56},{56,64},{64,7... | collective-permute-start | bytes 73736 | tf_op jit(solution)/shard_map/ppermute | solution.py:15
  70.4 12.1 %collective-permute-start.3 = (f32[3,8,1,128]{3,1,2,0:T(8,128)S(1)}, f32[3,8,1,128]{3,1,2,0:T(8,128)S(1)}, u32[]{:S(2)}, u32[]{:S(2)}) collective-permute-start(f32[3,8,1,128]{3,1,2,0:T(8,128)S(1)} %get-tuple-element.34), channel_id=1, source_target_pairs={{1,0},{2,1},{3,2},{4,3},{5,4},{6,5},{7,6},{9,8},{10,9},{11,10},{12... | collective-permute-start | bytes 36872 | tf_op jit(solution)/shard_map/ppermute | solution.py:18
  82.5 1.9 collective-permute-start.2
  88.7 4.6 collective-permute-start.4
  94.1 2.9 collective-permute-start.7
  97.1 3.7 collective-permute-start.6
  106.0 4.5 collective-permute-start.8
  111.4 1.9 collective-permute-start.11
  113.3 5.0 %collective-permute-start.10 = (f32[1,8,1,128]{3,1,2,0:T(8,128)S(1)}, f32[1,8,1,128]{3,1,2,0:T(8,128)S(1)}, u32[]{:S(2)}, u32[]{:S(2)}) collective-permute-start(f32[1,8,1,128]{3,1,2,0:T(8,128)S(1)} %get-tuple-element.47), channel_id=1, source_target_pairs={{0,1},{1,2},{2,3},{3,4},{4,5},{5,6},{6,7},{8,9},{9,10},{10,11},{11... | collective-permute-start | bytes 12296 | tf_op jit(solution)/shard_map/ppermute | solution.py:15
  119.9 119.6 %all-reduce.7 = (f32[]{:T(128)}, f32[]{:T(128)}) all-reduce(f32[]{:T(128)} %get-tuple-element.14, f32[]{:T(128)} %get-tuple-element.13), channel_id=1, replica_groups=mesh['wide'=96,'narrow'=8] {'wide','narrow'}, use_global_device_ids=true, to_apply=%region_1.2 | all-reduce | flops 2 | bytes 16 | tf_op jit(solution)/shard_map/psum | solution.py:118
  245.1 4.3 collective-permute-start.12
  250.2 3.4 collective-permute-start.15
  253.7 2.8 collective-permute-start.14
  258.1 109.1 %all-reduce.6 = (f32[]{:T(128)}, f32[]{:T(128)}) all-reduce(f32[]{:T(128)} %get-tuple-element.12, f32[]{:T(128)} %get-tuple-element.11), channel_id=1, replica_groups=mesh['wide'=96,'narrow'=8] {'wide','narrow'}, use_global_device_ids=true, to_apply=%region_5.6 | all-reduce | flops 2 | bytes 16 | tf_op jit(solution)/shard_map/psum | solution.py:118
  374.4 1.3 collective-permute-start.17
  375.7 4.3 collective-permute-start.16
  380.9 3.4 collective-permute-start.19
  384.3 3.5 collective-permute-start.18
  389.4 109.0 %all-reduce.5 = (f32[]{:T(128)}, f32[]{:T(128)}) all-reduce(f32[]{:T(128)} %get-tuple-element.10, f32[]{:T(128)} %get-tuple-element.9), channel_id=1, replica_groups=mesh['wide'=96,'narrow'=8] {'wide','narrow'}, use_global_device_ids=true, to_apply=%region_9.10 | all-reduce | flops 2 | bytes 16 | tf_op jit(solution)/shard_map/psum | solution.py:118
  (156 shorter events, 36.8 us)
Async XLA Ops:
  2.7 4.3 copy-start.12
  25.6 1.2 copy-start.3
  31.0 1.3 copy-start.17
  31.0 1.4 copy-start.16
  32.4 1.3 copy-start.15
  60.4 9.1 %copy-start.1 = (f32[8,16,128]{2,0,1:T(8,128)S(1)}, f32[8,16,128]{2,0,1:T(8,128)}, u32[]{:S(2)}) copy-start(f32[8,16,128]{2,0,1:T(8,128)} %constant.155.clone) | copy-start | bytes 196612
  60.4 25.3 %copy-start.4 = (f32[3,8,16,128]{3,2,1,0:T(8,128)S(1)}, f32[3,8,16,128]{3,2,1,0:T(8,128)}, u32[]{:S(2)}) copy-start(f32[3,8,16,128]{3,2,1,0:T(8,128)} %param.11) | copy-start | bytes 589828
  62.6 7.0 %collective-permute-start.1 = (f32[3,1,16,128]{3,1,2,0:T(1,128)S(1)}, f32[3,1,16,128]{3,1,2,0:T(1,128)S(1)}, u32[]{:S(2)}, u32[]{:S(2)}) collective-permute-start(f32[3,1,16,128]{3,1,2,0:T(1,128)S(1)} %get-tuple-element.36), channel_id=1, source_target_pairs={{8,0},{16,8},{24,16},{32,24},{40,32},{48,40},{56,48},{64,56},{72,6... | collective-permute-start | bytes 73736 | tf_op jit(solution)/shard_map/ppermute | solution.py:18
  63.9 6.4 %collective-permute-start = (f32[3,1,16,128]{3,1,2,0:T(1,128)S(1)}, f32[3,1,16,128]{3,1,2,0:T(1,128)S(1)}, u32[]{:S(2)}, u32[]{:S(2)}) collective-permute-start(f32[3,1,16,128]{3,1,2,0:T(1,128)S(1)} %get-tuple-element.35), channel_id=1, source_target_pairs={{0,8},{8,16},{16,24},{24,32},{32,40},{40,48},{48,56},{56,64},{64,7... | collective-permute-start | bytes 73736 | tf_op jit(solution)/shard_map/ppermute | solution.py:15
  70.4 15.7 %copy-start.7 = (f32[8,8,1,1]{1,0,3,2:T(8,128)S(1)}, f32[8,8,1,1]{1,0,3,2:T(8,128)}, u32[]{:S(2)}) copy-start(f32[8,8,1,1]{1,0,3,2:T(8,128)} %constant.190) | copy-start | bytes 772
  70.4 14.0 %collective-permute-start.3 = (f32[3,8,1,128]{3,1,2,0:T(8,128)S(1)}, f32[3,8,1,128]{3,1,2,0:T(8,128)S(1)}, u32[]{:S(2)}, u32[]{:S(2)}) collective-permute-start(f32[3,8,1,128]{3,1,2,0:T(8,128)S(1)} %get-tuple-element.34), channel_id=1, source_target_pairs={{1,0},{2,1},{3,2},{4,3},{5,4},{6,5},{7,6},{9,8},{10,9},{11,10},{12... | collective-permute-start | bytes 36872 | tf_op jit(solution)/shard_map/ppermute | solution.py:18
  82.5 3.1 collective-permute-start.2
  85.9 1.2 copy-start.9
  87.1 15.0 %copy-start = (f32[8,16,16,8]{2,3,1,0:T(8,128)S(1)}, f32[8,16,16,8]{2,3,1,0:T(8,128)}, u32[]{:S(2)}) copy-start(f32[8,16,16,8]{2,3,1,0:T(8,128)} %constant.172) | copy-start | bytes 196612
  87.4 5.9 %collective-permute-start.5 = (f32[1,1,16,128]{3,1,2,0:T(1,128)S(1)}, f32[1,1,16,128]{3,1,2,0:T(1,128)S(1)}, u32[]{:S(2)}, u32[]{:S(2)}) collective-permute-start(f32[1,1,16,128]{3,1,2,0:T(1,128)S(1)} %get-tuple-element.54), channel_id=1, source_target_pairs={{8,0},{16,8},{24,16},{32,24},{40,32},{48,40},{56,48},{64,56},{72,6... | collective-permute-start | bytes 24584 | tf_op jit(solution)/shard_map/ppermute | solution.py:18
  88.7 5.3 %collective-permute-start.4 = (f32[1,1,16,128]{3,1,2,0:T(1,128)S(1)}, f32[1,1,16,128]{3,1,2,0:T(1,128)S(1)}, u32[]{:S(2)}, u32[]{:S(2)}) collective-permute-start(f32[1,1,16,128]{3,1,2,0:T(1,128)S(1)} %get-tuple-element.53), channel_id=1, source_target_pairs={{0,8},{8,16},{16,24},{24,32},{32,40},{40,48},{48,56},{56,64},{64,7... | collective-permute-start | bytes 24584 | tf_op jit(solution)/shard_map/ppermute | solution.py:15
  94.1 6.7 %collective-permute-start.7 = (f32[1,8,1,128]{3,1,2,0:T(8,128)S(1)}, f32[1,8,1,128]{3,1,2,0:T(8,128)S(1)}, u32[]{:S(2)}, u32[]{:S(2)}) collective-permute-start(f32[1,8,1,128]{3,1,2,0:T(8,128)S(1)} %get-tuple-element.52), channel_id=1, source_target_pairs={{1,0},{2,1},{3,2},{4,3},{5,4},{6,5},{7,6},{9,8},{10,9},{11,10},{12... | collective-permute-start | bytes 12296 | tf_op jit(solution)/shard_map/ppermute | solution.py:18
  97.1 4.5 collective-permute-start.6
  103.0 1.4 copy-start.5
  103.1 1.4 copy-start.10
  104.7 5.8 %collective-permute-start.9 = (f32[1,1,16,128]{3,1,2,0:T(1,128)S(1)}, f32[1,1,16,128]{3,1,2,0:T(1,128)S(1)}, u32[]{:S(2)}, u32[]{:S(2)}) collective-permute-start(f32[1,1,16,128]{3,1,2,0:T(1,128)S(1)} %get-tuple-element.50), channel_id=1, source_target_pairs={{8,0},{16,8},{24,16},{32,24},{40,32},{48,40},{56,48},{64,56},{72,6... | collective-permute-start | bytes 24584 | tf_op jit(solution)/shard_map/ppermute | solution.py:18
  106.0 5.3 %collective-permute-start.8 = (f32[1,1,16,128]{3,1,2,0:T(1,128)S(1)}, f32[1,1,16,128]{3,1,2,0:T(1,128)S(1)}, u32[]{:S(2)}, u32[]{:S(2)}) collective-permute-start(f32[1,1,16,128]{3,1,2,0:T(1,128)S(1)} %get-tuple-element.49), channel_id=1, source_target_pairs={{0,8},{8,16},{16,24},{24,32},{32,40},{40,48},{48,56},{56,64},{64,7... | collective-permute-start | bytes 24584 | tf_op jit(solution)/shard_map/ppermute | solution.py:15
  111.4 7.0 %collective-permute-start.11 = (f32[1,8,1,128]{3,1,2,0:T(8,128)S(1)}, f32[1,8,1,128]{3,1,2,0:T(8,128)S(1)}, u32[]{:S(2)}, u32[]{:S(2)}) collective-permute-start(f32[1,8,1,128]{3,1,2,0:T(8,128)S(1)} %get-tuple-element.48), channel_id=1, source_target_pairs={{1,0},{2,1},{3,2},{4,3},{5,4},{6,5},{7,6},{9,8},{10,9},{11,10},{12... | collective-permute-start | bytes 12296 | tf_op jit(solution)/shard_map/ppermute | solution.py:18
  113.3 5.8 %collective-permute-start.10 = (f32[1,8,1,128]{3,1,2,0:T(8,128)S(1)}, f32[1,8,1,128]{3,1,2,0:T(8,128)S(1)}, u32[]{:S(2)}, u32[]{:S(2)}) collective-permute-start(f32[1,8,1,128]{3,1,2,0:T(8,128)S(1)} %get-tuple-element.47), channel_id=1, source_target_pairs={{0,1},{1,2},{2,3},{3,4},{4,5},{5,6},{6,7},{8,9},{9,10},{10,11},{11... | collective-permute-start | bytes 12296 | tf_op jit(solution)/shard_map/ppermute | solution.py:15
  243.8 5.6 %collective-permute-start.13 = (f32[1,1,16,128]{3,1,2,0:T(1,128)S(1)}, f32[1,1,16,128]{3,1,2,0:T(1,128)S(1)}, u32[]{:S(2)}, u32[]{:S(2)}) collective-permute-start(f32[1,1,16,128]{3,1,2,0:T(1,128)S(1)} %get-tuple-element.46), channel_id=1, source_target_pairs={{8,0},{16,8},{24,16},{32,24},{40,32},{48,40},{56,48},{64,56},{72,6... | collective-permute-start | bytes 24584 | tf_op jit(solution)/shard_map/ppermute | solution.py:18
  245.1 5.1 %collective-permute-start.12 = (f32[1,1,16,128]{3,1,2,0:T(1,128)S(1)}, f32[1,1,16,128]{3,1,2,0:T(1,128)S(1)}, u32[]{:S(2)}, u32[]{:S(2)}) collective-permute-start(f32[1,1,16,128]{3,1,2,0:T(1,128)S(1)} %get-tuple-element.45), channel_id=1, source_target_pairs={{0,8},{8,16},{16,24},{24,32},{32,40},{40,48},{48,56},{56,64},{64,7... | collective-permute-start | bytes 24584 | tf_op jit(solution)/shard_map/ppermute | solution.py:15
  250.2 6.2 %collective-permute-start.15 = (f32[1,8,1,128]{3,1,2,0:T(8,128)S(1)}, f32[1,8,1,128]{3,1,2,0:T(8,128)S(1)}, u32[]{:S(2)}, u32[]{:S(2)}) collective-permute-start(f32[1,8,1,128]{3,1,2,0:T(8,128)S(1)} %get-tuple-element.44), channel_id=1, source_target_pairs={{1,0},{2,1},{3,2},{4,3},{5,4},{6,5},{7,6},{9,8},{10,9},{11,10},{12... | collective-permute-start | bytes 12296 | tf_op jit(solution)/shard_map/ppermute | solution.py:18
  253.7 3.5 collective-permute-start.14
  374.4 5.6 %collective-permute-start.17 = (f32[1,1,16,128]{3,1,2,0:T(1,128)S(1)}, f32[1,1,16,128]{3,1,2,0:T(1,128)S(1)}, u32[]{:S(2)}, u32[]{:S(2)}) collective-permute-start(f32[1,1,16,128]{3,1,2,0:T(1,128)S(1)} %get-tuple-element.42), channel_id=1, source_target_pairs={{8,0},{16,8},{24,16},{32,24},{40,32},{48,40},{56,48},{64,56},{72,6... | collective-permute-start | bytes 24584 | tf_op jit(solution)/shard_map/ppermute | solution.py:18
  375.7 5.1 %collective-permute-start.16 = (f32[1,1,16,128]{3,1,2,0:T(1,128)S(1)}, f32[1,1,16,128]{3,1,2,0:T(1,128)S(1)}, u32[]{:S(2)}, u32[]{:S(2)}) collective-permute-start(f32[1,1,16,128]{3,1,2,0:T(1,128)S(1)} %get-tuple-element.41), channel_id=1, source_target_pairs={{0,8},{8,16},{16,24},{24,32},{32,40},{40,48},{48,56},{56,64},{64,7... | collective-permute-start | bytes 24584 | tf_op jit(solution)/shard_map/ppermute | solution.py:15
  380.9 7.7 %collective-permute-start.19 = (f32[1,8,1,128]{3,1,2,0:T(8,128)S(1)}, f32[1,8,1,128]{3,1,2,0:T(8,128)S(1)}, u32[]{:S(2)}, u32[]{:S(2)}) collective-permute-start(f32[1,8,1,128]{3,1,2,0:T(8,128)S(1)} %get-tuple-element.40), channel_id=1, source_target_pairs={{1,0},{2,1},{3,2},{4,3},{5,4},{6,5},{7,6},{9,8},{10,9},{11,10},{12... | collective-permute-start | bytes 12296 | tf_op jit(solution)/shard_map/ppermute | solution.py:18
  384.3 4.3 collective-permute-start.18
  (8 other events, 7.6 us)
where the time goes:
time: 514 us; the launch traced here: 504 us
  blocking collectives  338 us (66%)
  starting transfers between devices  70.4 us (14%)
  matrix products  49 us (10%)
  local copies, waits for them, and re-layouts  24.3 us (5%)
  between operations  11.7 us (2%)
  waiting for transfers between devices  7.04 us (1%)
    psum x3, blocking collectives, merged_dots(): lax.psum((jnp.sum(first * first * inverse_mult), jnp.sum(second * first *...  338 us
    dot_general x33, matrix products, along_axis(): result = jnp.einsum(form, split, matrix, precision=highest)  49 us
    ppermute x10, starting transfers between devices, padded_2(): lax.ppermute(lax.slice_in_dim(block, block.shape[dim] - width, None, axis...  40.1 us
    ppermute x10, starting transfers between devices, padded_2(): lax.ppermute(lax.slice_in_dim(block, 0, width, axis=dim), axis, backward)  30.3 us
  transfers between devices with their start and end apart: 20, of which 9 were waited for; matrix products, arithmetic and copies ran while one was open for 0% of the time, Pallas kernels for 0%

commit v1 on v0

v1 whole, which is shorter than its diff:
```python
import functools

import jax
import jax.numpy as jnp
import ml_dtypes
import numpy as np
from jax import lax
from jax.experimental import pallas as pl
from jax.experimental.pallas import tpu as pltpu
from jax.sharding import PartitionSpec as P

MESH = pl.DeviceIdType.MESH
SHIFT = 4.0
SIDES = ((1, 0), (-1, 0), (0, 1), (0, -1), (1, 1), (1, -1), (-1, 1), (-1, -1))


def legendre_pair(order, nodes):
    p_prev = np.ones(nodes.shape)
    p_now = nodes * 1.0
    for k in range(2, order + 1):
        p_next = ((2 * k - 1) * nodes * p_now - (k - 1) * p_prev) / k
        p_prev = p_now
        p_now = p_next
    return (p_now, p_prev)


def spectral_tables():
    degree = 7
    points = degree + 1
    gll_nodes = np.cos(np.pi * np.arange(points) / degree)
    for sweep in range(100):
        p_now, p_prev = legendre_pair(degree, gll_nodes)
        gll_nodes = gll_nodes - (gll_nodes * p_now - p_prev) / ((degree + 1) * p_now)
    gll_nodes = np.sort(gll_nodes)
    legendre_vals, unused_prev = legendre_pair(degree, gll_nodes)
    gll_weights = 2.0 / (degree * (degree + 1) * legendre_vals**2)
    derivative = np.zeros((points, points))
    for row_index in range(points):
        for col_index in range(points):
            if row_index != col_index:
                derivative[row_index, col_index] = legendre_vals[row_index] / (
                    legendre_vals[col_index] * (gll_nodes[row_index] - gll_nodes[col_index])
                )
    derivative[0, 0] = -degree * (degree + 1) / 4.0
    derivative[-1, -1] = degree * (degree + 1) / 4.0
    gauss_nodes = np.cos(np.pi * (np.arange(12) + 0.75) / 12.5)
    for sweep in range(100):
        p_now, p_prev = legendre_pair(12, gauss_nodes)
        slope = 12 * (gauss_nodes * p_now - p_prev) / (gauss_nodes * gauss_nodes - 1.0)
        gauss_nodes = gauss_nodes - p_now / slope
    gauss_nodes = np.sort(gauss_nodes)
    p_now, p_prev = legendre_pair(12, gauss_nodes)
    slope = 12 * (gauss_nodes * p_now - p_prev) / (gauss_nodes * gauss_nodes - 1.0)
    gauss_weights = 2.0 / ((1.0 - gauss_nodes**2) * slope**2)
    interpolate = np.ones((12, points))
    for col_index in range(points):
        for other in range(points):
            if other != col_index:
                interpolate[:, col_index] *= (gauss_nodes - gll_nodes[other]) / (
                    gll_nodes[col_index] - gll_nodes[other]
                )
    return (gll_weights, derivative, gauss_weights, interpolate)


def halves(matrix):
    high = matrix.astype(ml_dtypes.bfloat16)
    low = (matrix - high.astype(np.float64)).astype(ml_dtypes.bfloat16)
    return high, low


def left_factor(matrix):
    high, low = halves(matrix)
    return np.concatenate([high, high, low], axis=1)


def right_factor(matrix):
    high, low = halves(matrix)
    return np.concatenate([high, high, low], axis=0)


def tables_for(len_z):
    weights, deriv, fine_weights, interp = spectral_tables()
    els_z = len_z // 8
    gradint = interp @ deriv
    stiff = deriv.T @ np.diag(weights) @ deriv
    eye2, eye_z = np.eye(2), np.eye(els_z)

    def shared(count):
        total = np.eye(8 * count)
        for k in range(count - 1):
            total[8 * k + 7, 8 * k + 8] = total[8 * k + 8, 8 * k + 7] = 1.0
        return total

    sum_y, sum_z = shared(2), shared(els_z)
    w_x, w_y, w_z = weights, np.tile(weights, 2), np.tile(weights, els_z)
    w_y2, w_z2 = sum_y @ w_y, sum_z @ w_z

    fine_z = np.zeros((len_z, 2 * 16 * els_z))
    back_z = np.zeros((16 * els_z, len_z))
    for e in range(els_z):
        fine_z[8 * e : 8 * e + 8, 16 * e : 16 * e + 12] = interp.T
        first = 16 * els_z + 16 * e
        fine_z[8 * e : 8 * e + 8, first : first + 12] = gradint.T
        back_z[16 * e : 16 * e + 12, 8 * e : 8 * e + 8] = fine_weights[:, None] * interp
    back_z = back_z @ sum_z
    fine_xy = np.concatenate(
        [np.kron(interp, interp), np.kron(gradint, interp), np.kron(interp, gradint)], axis=0
    )
    back = interp.T * fine_weights[None, :]
    back_xy = np.kron(back, back)

    op_xy = np.kron(stiff, np.diag(w_y2)) + np.kron(np.diag(w_x), sum_y @ np.kron(eye2, stiff))
    op_z = np.kron(eye_z, stiff).T @ sum_z
    weak = np.diag(weights) @ deriv
    div_xy = np.concatenate(
        [np.kron(weak, np.diag(w_y)), np.kron(np.diag(w_x), np.kron(eye2, weak))], axis=1
    )
    div_xy2 = np.concatenate(
        [np.kron(weak, np.diag(w_y2)), np.kron(np.diag(w_x), sum_y @ np.kron(eye2, weak))], axis=1
    )
    div_z = np.kron(eye_z, weak).T
    div_z2 = div_z @ sum_z

    w_xy, w_xy2 = np.kron(w_x, w_y), np.kron(w_x, w_y2)
    half_y = 1.0 / (sum_y @ np.ones(16))
    half_z = 1.0 / (sum_z @ np.ones(len_z))
    ones_x, ones_z = np.ones(8), np.ones(len_z)
    plain = np.stack(
        [
            np.outer(w_xy, w_z),
            np.outer(w_xy, ones_z),
            np.outer(w_xy2, ones_z),
            1.0 / np.outer(w_xy2, w_z2),
            np.outer(np.kron(ones_x, half_y), half_z),
            np.outer(np.ones(128), w_z),
            np.outer(np.ones(128), w_z2),
        ]
    ).astype(np.float32)
    from_right = np.concatenate(
        [right_factor(back_z), right_factor(op_z), right_factor(div_z), right_factor(div_z2)], axis=0
    )
    from_left = np.concatenate(
        [left_factor(op_xy), left_factor(div_xy), left_factor(div_xy2)], axis=1
    )
    return (
        right_factor(fine_z),
        left_factor(fine_xy),
        from_right,
        from_left,
        left_factor(back_xy),
        plain,
    )


def split(value):
    high = value.astype(jnp.bfloat16)
    low = (value - high.astype(jnp.float32)).astype(jnp.bfloat16)
    return high, low


def stacked(value):
    high, low = split(value)
    return jnp.concatenate([high, low, high], axis=0)


def joined(value):
    high, low = split(value)
    return jnp.concatenate([high, low, high], axis=1)


def mul(first, second):
    return jnp.dot(first, second, preferred_element_type=jnp.float32)


def kernel(
    sizes,
    vel_hbm,
    rea_hbm,
    fine_z_hbm,
    fine_xy_hbm,
    right_hbm,
    left_hbm,
    back_xy_hbm,
    plain_hbm,
    adv_ref,
    pres_ref,
    resid_ref,
    vel_ref,
    rea_ref,
    fine_z_ref,
    fine_xy_ref,
    right_ref,
    left_ref,
    back_xy_ref,
    plain_ref,
    load_sem,
    adv_q,
    ops_q,
    sx3,
    sy3,
    sc3,
    rx3,
    ry3,
    rc3,
    sx1,
    sy1,
    sc1,
    rx1,
    ry1,
    rc1,
    part,
    got,
    send_sem,
    recv_sem,
    tree_send,
    tree_recv,
):
    pairs = (
        (vel_hbm, vel_ref),
        (fine_z_hbm, fine_z_ref),
        (fine_xy_hbm, fine_xy_ref),
        (right_hbm, right_ref),
        (back_xy_hbm, back_xy_ref),
        (plain_hbm, plain_ref),
        (rea_hbm, rea_ref),
        (left_hbm, left_ref),
    )
    loads = [pltpu.make_async_copy(a, b, load_sem.at[k]) for k, (a, b) in enumerate(pairs)]
    for load in loads:
        load.start()

    count_x, count_y, low_count = sizes
    high_count = count_x // low_count
    me_x, me_y = lax.axis_index("wide"), lax.axis_index("narrow")
    me_low, me_high = lax.rem(me_x, low_count), me_x // low_count

    def at_side(side):
        return (
            lax.rem(me_x + (side[0] + count_x), count_x),
            lax.rem(me_y + (side[1] + count_y), count_y),
        )

    stages = (
        [(me_x, lax.rem(me_y + d, count_y)) for d in range(1, count_y)],
        [
            (me_high * low_count + lax.rem(me_low + d, low_count), me_y)
            for d in range(1, low_count)
        ],
        [
            (lax.rem(me_high + d, high_count) * low_count + me_low, me_y)
            for d in range(1, high_count)
        ],
    )
    partners = [at_side(side) for side in SIDES] + [who for stage in stages for who in stage]

    barrier = pltpu.get_barrier_semaphore()
    for who in partners:
        pl.semaphore_signal(barrier, inc=1, device_id=who, device_id_type=MESH)

    for load in loads[:3]:
        load.wait()
    parts = []
    for c in range(3):
        for e in range(2):
            parts.append(vel_ref[c, :, 8 * e : 8 * e + 8, :].reshape(64, 128))
    on_z = mul(joined(jnp.concatenate(parts, axis=0)), fine_z_ref[...])
    width = on_z.shape[1] // 2
    products = {}
    for e in range(2):
        fine = []
        for c in range(3):
            first = 64 * (2 * c + e)
            flat = mul(fine_xy_ref[...], stacked(on_z[first : first + 64, :width]))
            steep = mul(fine_xy_ref[:144, :], stacked(on_z[first : first + 64, width:]))
            fine.append((flat[:144], flat[144:288], flat[288:], steep))
        for c in range(3):
            products[c, e] = (
                fine[0][0] * fine[c][1] + fine[1][0] * fine[c][2] + fine[2][0] * fine[c][3]
            )
    for load in loads[3:5]:
        load.wait()
    row8 = lax.broadcasted_iota(jnp.int32, (8, 8, 128), 1)
    back_rows = 3 * width
    for c in range(3):
        both = []
        for e in range(2):
            both.append(stacked(mul(joined(products[c, e]), right_ref[:back_rows, :])))
        weak = mul(back_xy_ref[...], jnp.concatenate(both, axis=1))
        first = weak[:, :128].reshape(8, 8, 128)
        second = weak[:, 128:].reshape(8, 8, 128)
        first, second = (
            first + jnp.where(row8 == 7, pltpu.roll(second, 7, 1), 0.0),
            second + jnp.where(row8 == 0, pltpu.roll(first, 1, 1), 0.0),
        )
        adv_q[c] = jnp.concatenate([first, second], axis=1).reshape(128, 128)

    pl.semaphore_wait(barrier, len(partners))

    has = {1: (me_x > 0, me_y > 0), -1: (me_x < count_x - 1, me_y < count_y - 1)}

    def exchange(q_ref, slots, bufs, index, comps):
        sx, sy, sc, rx, ry, rc = bufs
        for c in range(comps):
            q = q_ref.at[c]
            sx[0, c] = q[112:128, :]
            sx[1, c] = q[0:16, :]
            sy[0, c] = q[pl.ds(15, 8, stride=16), :]
            sy[1, c] = q[pl.ds(0, 8, stride=16), :]
            for k, row in enumerate((127, 112, 15, 0)):
                sc[k, c : c + 1, :] = q[row : row + 1, :]
        copies = []
        for k, side in enumerate(SIDES):
            if k < 2:
                source, target = sx.at[k], rx.at[k]
            elif k < 4:
                source, target = sy.at[k - 2], ry.at[k - 2]
            else:
                source, target = sc.at[k - 4], rc.at[k - 4]
            copies.append(
                pltpu.make_async_remote_copy(
                    src_ref=source,
                    dst_ref=target,
                    send_sem=send_sem.at[index, k],
                    recv_sem=recv_sem.at[index, k],
                    device_id=at_side(side),
                    device_id_type=MESH,
                )
            )
        for copy in copies:
            copy.start()
        return copies

    row_x = lax.broadcasted_iota(jnp.int32, (8, 128), 0)

    def receive(q_ref, bufs, copies, comps):
        sx, sy, sc, rx, ry, rc = bufs
        for copy in copies:
            copy.wait_recv()
        for c in range(comps):
            q = q_ref.at[c]
            q[0:16, :] = q[0:16, :] + jnp.where(has[1][0], rx[0, c], 0.0)
            q[112:128, :] = q[112:128, :] + jnp.where(has[-1][0], rx[1, c], 0.0)
            for k, step in ((0, 1), (1, -1)):
                line = ry[k, c]
                low = jnp.where(has[1][0], rc[k, c : c + 1, :], 0.0)
                high = jnp.where(has[-1][0], rc[2 + k, c : c + 1, :], 0.0)
                line = line + jnp.where(row_x == 0, low, 0.0) + jnp.where(row_x == 7, high, 0.0)
                rows = pl.ds(0 if step == 1 else 15, 8, stride=16)
                q[rows, :] = q[rows, :] + jnp.where(has[step][1], line, 0.0)

    three = (sx3, sy3, sc3, rx3, ry3, rc3)
    ones = [tuple(buf.at[k] for buf in (sx1, sy1, sc1, rx1, ry1, rc1)) for k in range(4)]
    copies = exchange(adv_q, None, three, 0, 3)
    flights = list(copies)

    for load in loads[5:]:
        load.wait()
    rows = lax.broadcasted_iota(jnp.int32, (128, 128), 0)
    in_x, in_y = rows // 16, lax.rem(rows, 16)
    lane = lax.broadcasted_iota(jnp.int32, (128, 128), 1)
    in_z = lax.rem(lane, 8)
    cross_x = ((in_x == 0) & has[1][0]) | ((in_x == 7) & has[-1][0])
    cross_y = ((in_y == 0) & has[1][1]) | ((in_y == 15) & has[-1][1])
    cross = jnp.where(cross_x, 0.5, 1.0) * jnp.where(cross_y, 0.5, 1.0)
    local_half = plain_ref[4]
    inverse_mult = cross * local_half
    inverse_mass = plain_ref[3] * cross

    def sum_yz(value):
        up = pltpu.roll(value, 1, 1)
        down = pltpu.roll(value, 127, 1)
        value = value + jnp.where((in_z == 0) & (lane > 0), up, 0.0)
        value = value + jnp.where((in_z == 7) & (lane < 127), down, 0.0)
        up = pltpu.roll(value, 1, 0)
        down = pltpu.roll(value, 127, 0)
        return value + jnp.where(in_y == 8, up, 0.0) + jnp.where(in_y == 7, down, 0.0)

    mass_term = sum_yz(plain_ref[0] * rea_ref[...].reshape(128, 128)) - SHIFT * cross
    vel = [vel_ref[c].reshape(128, 128) for c in range(3)]
    op_xy, div_xy, div_xy2 = (slice(0, 384), slice(384, 1152), slice(1152, 1920))
    op_z, div_z, div_z2 = (slice(back_rows + 384 * k, back_rows + 384 * k + 384) for k in range(3))

    def divergence(field, on_xy, on_z, scale_z, scale_xy):
        flat = mul(left_ref[:, on_xy], stacked(jnp.concatenate(field[:2], axis=0)))
        return scale_z * flat + scale_xy * mul(joined(field[2]), right_ref[on_z, :])

    base = sum_yz(divergence(vel, div_xy, div_z, plain_ref[5], plain_ref[1]))

    def operate(value):
        flat = mul(left_ref[:, op_xy], stacked(value))
        along = mul(joined(value), right_ref[op_z, :])
        return plain_ref[6] * flat + plain_ref[2] * along + mass_term * value

    receive(adv_q, three, copies, 3)
    adv = []
    for c in range(3):
        adv.append(adv_q[c] * inverse_mass)
    ops_q[0] = 0.05 * divergence(adv, div_xy2, div_z2, plain_ref[6], plain_ref[2]) - base
    copies = exchange(ops_q.at[pl.ds(0, 1)], None, ones[0], 1, 1)
    flights += copies
    for c in range(3):
        adv_ref[c] = adv[c].reshape(8, 16, 128)
    receive(ops_q.at[pl.ds(0, 1)], ones[0], copies, 1)

    def dot(first, second, scale):
        return jnp.sum(first * second * scale, axis=0, keepdims=True)

    z0 = ops_q[0]
    ops_q[1] = operate(z0)
    copies = exchange(ops_q.at[pl.ds(1, 1)], None, ones[1], 2, 1)
    flights += copies
    part[0, 0:1, :] = dot(z0, z0, inverse_mult)
    part[0, 6:8, :] = jnp.zeros((2, 128), jnp.float32)
    receive(ops_q.at[pl.ds(1, 1)], ones[1], copies, 1)
    z1 = ops_q[1]
    ops_q[2] = operate(z1)
    copies = exchange(ops_q.at[pl.ds(2, 1)], None, ones[2], 3, 1)
    flights += copies
    part[0, 1:2, :] = dot(z0, z1, inverse_mult)
    part[0, 2:3, :] = dot(z1, z1, inverse_mult)
    receive(ops_q.at[pl.ds(2, 1)], ones[2], copies, 1)
    z2 = ops_q[2]
    last = operate(z2)
    part[0, 3:4, :] = dot(z1, z2, inverse_mult)
    part[0, 4:5, :] = dot(z2, z2, inverse_mult)
    part[0, 5:6, :] = dot(z2, last, local_half)

    slot = 0
    for index, stage in enumerate(stages):
        copies_in = []
        for k, who in enumerate(stage):
            copies_in.append(
                pltpu.make_async_remote_copy(
                    src_ref=part.at[index],
                    dst_ref=got.at[slot + k],
                    send_sem=tree_send.at[slot + k],
                    recv_sem=tree_recv.at[slot + k],
                    device_id=who,
                    device_id_type=MESH,
                )
            )
        for copy in copies_in:
            copy.start()
        if index == 0:
            ops_q[3] = last
            copies = exchange(ops_q.at[pl.ds(3, 1)], None, ones[3], 4, 1)
            flights += copies
        for copy in copies_in:
            copy.wait_recv()
        total = part[index]
        for k in range(len(stage)):
            total = total + got[slot + k]
        if index < 2:
            part[index + 1] = total
        flights += copies_in
        slot += len(stage)

    receive(ops_q.at[pl.ds(3, 1)], ones[3], copies, 1)
    sums = jnp.broadcast_to(jnp.sum(total, axis=1, keepdims=True), (8, 128))
    g00, g01, g11, g12, g22, g23 = (sums[k : k + 1, :] for k in range(6))
    h00 = g01 + SHIFT * g00
    h01 = g11 + SHIFT * g01
    h11 = g12 + SHIFT * g11
    h02 = g12 + SHIFT * g11
    h12 = g22 + SHIFT * g12
    h22 = g23 + SHIFT * g22
    over = 1.0 / h00
    l10, l20 = h01 * over, h02 * over
    d1 = h11 - l10 * h01
    e1 = h12 - l10 * h02
    over1 = 1.0 / d1
    l21 = e1 * over1
    d2 = h22 - l20 * h02 - l21 * e1
    b1 = g01 - l10 * g00
    b2 = g11 - l20 * g00 - l21 * b1
    c2 = b2 / d2
    c1 = b1 * over1 - l21 * c2
    c0 = g00 * over - l10 * c1 - l20 * c2
    z3 = ops_q[3]
    pres = c0 * z0 + c1 * z1 + c2 * z2
    pres_ref[...] = pres.reshape(8, 16, 128)
    resid = (
        (1.0 - SHIFT * c0) * z0 - (c0 + SHIFT * c1) * z1 - (c1 + SHIFT * c2) * z2 - c2 * z3
    )
    resid_ref[...] = resid.reshape(8, 16, 128)
    for copy in flights:
        copy.wait_send()


def per_device(sizes, velocity, reaction):
    consts = [jnp.asarray(value) for value in tables_for(reaction.shape[2])]
    operands = [velocity, reaction] + consts
    shape_of = jax.ShapeDtypeStruct
    count_x, count_y, low_count = sizes
    trips = (count_y - 1) + (low_count - 1) + (count_x // low_count - 1)
    vmem, f32, dma = pltpu.VMEM, jnp.float32, pltpu.SemaphoreType.DMA
    return pl.pallas_call(
        functools.partial(kernel, sizes),
        out_shape=(
            shape_of(velocity.shape, f32),
            shape_of(reaction.shape, f32),
            shape_of(reaction.shape, f32),
        ),
        in_specs=[pl.BlockSpec(memory_space=pltpu.HBM)] * 8,
        out_specs=(pl.BlockSpec(memory_space=vmem),) * 3,
        scratch_shapes=[vmem(value.shape, value.dtype) for value in operands]
        + [
            dma((8,)),
            vmem((3, 128, 128), f32),
            vmem((4, 128, 128), f32),
            vmem((2, 3, 16, 128), f32),
            vmem((2, 3, 8, 128), f32),
            vmem((4, 8, 128), f32),
            vmem((2, 3, 16, 128), f32),
            vmem((2, 3, 8, 128), f32),
            vmem((4, 8, 128), f32),
            vmem((4, 2, 1, 16, 128), f32),
            vmem((4, 2, 1, 8, 128), f32),
            vmem((4, 4, 8, 128), f32),
            vmem((4, 2, 1, 16, 128), f32),
            vmem((4, 2, 1, 8, 128), f32),
            vmem((4, 4, 8, 128), f32),
            vmem((3, 8, 128), f32),
            vmem((trips, 8, 128), f32),
            dma((5, 8)),
            dma((5, 8)),
            dma((trips,)),
            dma((trips,)),
        ],
        compiler_params=pltpu.CompilerParams(
            collective_id=0, has_side_effects=True, vmem_limit_bytes=54700 * 1024
        ),
    )(*operands)


def solution(mesh):
    count_x, count_y = mesh.shape["wide"], mesh.shape["narrow"]
    low_count = 12 if count_x % 12 == 0 else 2
    return jax.shard_map(
        functools.partial(per_device, (count_x, count_y, low_count)),
        mesh=mesh,
        in_specs=(P(None, "wide", "narrow", None), P("wide", "narrow", None)),
        out_specs=(
            P(None, "wide", "narrow", None),
            P("wide", "narrow", None),
            P("wide", "narrow", None),
        ),
        check_vma=False,
    )
```

time: 514 us -> 54.7 us (0.11); the launches traced: 504 us -> 54.3 us
  blocking collectives: 338 us -> 0 us
  starting transfers between devices: 70.4 us -> 0 us
  Pallas kernels: 0 us -> 50.1 us
  matrix products: 49 us -> 0 us
  local copies, waits for them, and re-layouts: 24.3 us -> 3.61 us
  between operations: 11.7 us -> 0.65 us
  waiting for transfers between devices: 7.04 us -> 0 us
    psum x3 -> x0, blocking collectives: 338 us -> none  [merged_dots(): lax.psum((jnp.sum(first * first * inverse_mult), jnp.sum(second * first *...]
    ppermute x20 -> x0, starting transfers between devices: 70.4 us -> none  [the longest x10 40.1 us: padded_2(): lax.ppermute(lax.slice_in_dim(block, block.shape[dim] - width, None, axis...]
    pallas_call x0 -> x1, Pallas kernels: none -> 50.1 us  [per_device(): pl.pallas_call(functools.partial(kernel, sizes), out_shape=(shape_of(velo...]
    dot_general x33 -> x0, matrix products: 49 us -> none  [along_axis(): result = jnp.einsum(form, split, matrix, precision=highest)]
    dot_general x2 -> x0, local copies, waits for them, and re-layouts: 7.72 us -> none  [along_axis(): result = jnp.einsum(form, split, matrix, precision=highest)]
    ppermute x20 -> x0, waiting for transfers between devices: 7.04 us -> none  [the longest x10 7.01 us: padded_2(): lax.ppermute(lax.slice_in_dim(block, block.shape[dim] - width, None, axis...]
    another operation x6 -> x0, local copies, waits for them, and re-layouts: 5.67 us -> none  [the longest x3 4.93 us: along_axis(): values.reshape(shape[:axis_pos] + (blocks, inner_len) + shape[axis_pos +...]
  transfers between devices with their start and end apart: 20 -> 0, of which waited for: 9 -> 0; matrix products, arithmetic and copies ran while one was open for 0% -> 0% of each run, Pallas kernels for 0% -> 0%
where the time goes in v1:
time: 54.7 us; the launch traced here: 54.3 us
  Pallas kernels  50.1 us (92%)
  local copies, waits for them, and re-layouts  3.61 us (7%)
  between operations  0.65 us (1%)
    pallas_call x1, Pallas kernels, per_device(): pl.pallas_call(functools.partial(kernel, sizes), out_shape=(shape_of(velo...  50.1 us
    unnamed x7, local copies, waits for them, and re-layouts  3.61 us

profile of v1, /device:TPU:1, one launch (start us, length us, event | category | flops | bytes accessed | tf_op | source)
XLA Modules:
  0.0 54.3 jit_solution(15646971858170474454)
XLA Ops:
  0.6 0.0 copy-start
  0.6 0.8 %copy-done = f32[8,16,128]{2,1,0:T(8,128)S(1)} copy-done((f32[8,16,128]{2,1,0:T(8,128)S(1)}, f32[8,16,128]{2,1,0:T(8,128)}, u32[]{:S(2)}) %copy-start) | copy-done | bytes 65560
  1.5 0.0 copy-start.1
  1.5 0.8 %copy-done.1 = bf16[64,432]{1,0:T(8,128)(2,1)S(1)} copy-done((bf16[64,432]{1,0:T(8,128)(2,1)S(1)}, bf16[64,432]{1,0:T(8,128)(2,1)}, u32[]{:S(2)}) %copy-start.1) | copy-done | bytes 55320
  2.3 50.1 %shard_map.103 = (f32[3,8,16,128]{3,2,1,0:T(8,128)S(1)}, f32[8,16,128]{2,1,0:T(8,128)S(1)}, f32[8,16,128]{2,1,0:T(8,128)S(1)}) custom-call(f32[3,8,16,128]{3,2,1,0:T(8,128)} %vel_hbm.1, f32[8,16,128]{2,1,0:T(8,128)S(1)} %copy-done, bf16[384,512]{1,0:T(8,128)(2,1)} %constant.12.clone.fine_z_hbm, bf16[432,192]{1,0:T(8,128)(2,1)} %constant.13.clone.fine_xy_hbm, ...), custom_call_target="tpu_custom_call" | custom-call | tf_op jit(solution)/shard_map/pallas_call | solution.py:497
  52.4 0.7 %copy.14 = f32[3,8,16,128]{3,2,1,0:T(8,128)} copy(f32[3,8,16,128]{3,2,1,0:T(8,128)S(1)} %get-tuple-element.6) | data formatting | bytes 393216
  53.1 0.6 %copy.15 = f32[8,16,128]{2,1,0:T(8,128)} copy(f32[8,16,128]{2,1,0:T(8,128)S(1)} %get-tuple-element.7) | data formatting | bytes 131072
  53.7 0.6 %copy.16 = f32[8,16,128]{2,1,0:T(8,128)} copy(f32[8,16,128]{2,1,0:T(8,128)S(1)} %get-tuple-element.8) | data formatting | bytes 131072
Async XLA Ops:
  0.6 0.8 %copy-start = (f32[8,16,128]{2,1,0:T(8,128)S(1)}, f32[8,16,128]{2,1,0:T(8,128)}, u32[]{:S(2)}) copy-start(f32[8,16,128]{2,1,0:T(8,128)} %rea_hbm.1) | copy-start | bytes 196612
  1.5 0.8 %copy-start.1 = (bf16[64,432]{1,0:T(8,128)(2,1)S(1)}, bf16[64,432]{1,0:T(8,128)(2,1)}, u32[]{:S(2)}) copy-start(bf16[64,432]{1,0:T(8,128)(2,1)} %constant.16.clone.back_xy_hbm) | copy-start | bytes 165892

commit v2 on v1

--- a/solution.py
+++ b/solution.py
@@ -142,12 +142,14 @@
     from_left = np.concatenate(
         [left_factor(op_xy), left_factor(div_xy), left_factor(div_xy2)], axis=1
     )
+    shapes_xy = np.zeros((496, 432), ml_dtypes.bfloat16)
+    shapes_xy[:432, :192] = left_factor(fine_xy)
+    shapes_xy[432:] = left_factor(back_xy)
     return (
         right_factor(fine_z),
-        left_factor(fine_xy),
+        shapes_xy,
         from_right,
         from_left,
-        left_factor(back_xy),
         plain,
     )
 
@@ -180,7 +182,6 @@
     fine_xy_hbm,
     right_hbm,
     left_hbm,
-    back_xy_hbm,
     plain_hbm,
     adv_ref,
     pres_ref,
@@ -191,7 +192,6 @@
     fine_xy_ref,
     right_ref,
     left_ref,
-    back_xy_ref,
     plain_ref,
     load_sem,
     adv_q,
@@ -220,7 +220,6 @@
         (fine_z_hbm, fine_z_ref),
         (fine_xy_hbm, fine_xy_ref),
         (right_hbm, right_ref),
-        (back_xy_hbm, back_xy_ref),
         (plain_hbm, plain_ref),
         (rea_hbm, rea_ref),
         (left_hbm, left_ref),
@@ -233,22 +232,31 @@
     high_count = count_x // low_count
     me_x, me_y = lax.axis_index("wide"), lax.axis_index("narrow")
     me_low, me_high = lax.rem(me_x, low_count), me_x // low_count
+    me_pair, me_core = me_y // 2, lax.rem(me_y, 2)
+
+    def turn(place, step, count):
+        moved = place + step % count
+        return jnp.where(moved >= count, moved - count, moved)
 
     def at_side(side):
-        return (
-            lax.rem(me_x + (side[0] + count_x), count_x),
-            lax.rem(me_y + (side[1] + count_y), count_y),
-        )
+        return turn(me_x, side[0], count_x), turn(me_y, side[1], count_y)
+
+    def far_first(count_a, count_b):
+        hops = lambda step, count: min(step, count - step)
+        steps = [(i, j) for i in range(count_a) for j in range(count_b) if (i, j) != (0, 0)]
+        return sorted(steps, key=lambda s: -hops(s[0], count_a) - hops(s[1], count_b))
 
     stages = (
-        [(me_x, lax.rem(me_y + d, count_y)) for d in range(1, count_y)],
         [
-            (me_high * low_count + lax.rem(me_low + d, low_count), me_y)
-            for d in range(1, low_count)
+            (me_high * low_count + turn(me_low, i, low_count), me_pair * 2 + turn(me_core, j, 2))
+            for i, j in far_first(low_count, 2)
         ],
         [
-            (lax.rem(me_high + d, high_count) * low_count + me_low, me_y)
-            for d in range(1, high_count)
+            (
+                turn(me_high, i, high_count) * low_count + me_low,
+                turn(me_pair, j, count_y // 2) * 2 + me_core,
+            )
+            for i, j in far_first(high_count, count_y // 2)
         ],
     )
     partners = [at_side(side) for side in SIDES] + [who for stage in stages for who in stage]
@@ -270,14 +278,14 @@
         fine = []
         for c in range(3):
             first = 64 * (2 * c + e)
-            flat = mul(fine_xy_ref[...], stacked(on_z[first : first + 64, :width]))
-            steep = mul(fine_xy_ref[:144, :], stacked(on_z[first : first + 64, width:]))
+            flat = mul(fine_xy_ref[:432, :192], stacked(on_z[first : first + 64, :width]))
+            steep = mul(fine_xy_ref[:144, :192], stacked(on_z[first : first + 64, width:]))
             fine.append((flat[:144], flat[144:288], flat[288:], steep))
         for c in range(3):
             products[c, e] = (
                 fine[0][0] * fine[c][1] + fine[1][0] * fine[c][2] + fine[2][0] * fine[c][3]
             )
-    for load in loads[3:5]:
+    for load in loads[3:4]:
         load.wait()
     row8 = lax.broadcasted_iota(jnp.int32, (8, 8, 128), 1)
     back_rows = 3 * width
@@ -285,7 +293,7 @@
         both = []
         for e in range(2):
             both.append(stacked(mul(joined(products[c, e]), right_ref[:back_rows, :])))
-        weak = mul(back_xy_ref[...], jnp.concatenate(both, axis=1))
+        weak = mul(fine_xy_ref[432:, :], jnp.concatenate(both, axis=1))
         first = weak[:, :128].reshape(8, 8, 128)
         second = weak[:, 128:].reshape(8, 8, 128)
         first, second = (
@@ -326,7 +334,7 @@
                     device_id_type=MESH,
                 )
             )
-        for copy in copies:
+        for copy in copies[4:] + copies[:4]:
             copy.start()
         return copies
 
@@ -353,7 +361,7 @@
     copies = exchange(adv_q, None, three, 0, 3)
     flights = list(copies)
 
-    for load in loads[5:]:
+    for load in loads[4:]:
         load.wait()
     rows = lax.broadcasted_iota(jnp.int32, (128, 128), 0)
     in_x, in_y = rows // 16, lax.rem(rows, 16)
@@ -450,7 +458,7 @@
         total = part[index]
         for k in range(len(stage)):
             total = total + got[slot + k]
-        if index < 2:
+        if index < 1:
             part[index + 1] = total
         flights += copies_in
         slot += len(stage)
@@ -492,7 +500,7 @@
     operands = [velocity, reaction] + consts
     shape_of = jax.ShapeDtypeStruct
     count_x, count_y, low_count = sizes
-    trips = (count_y - 1) + (low_count - 1) + (count_x // low_count - 1)
+    trips = (2 * low_count - 1) + (count_x // low_count * count_y // 2 - 1)
     vmem, f32, dma = pltpu.VMEM, jnp.float32, pltpu.SemaphoreType.DMA
     return pl.pallas_call(
         functools.partial(kernel, sizes),
@@ -501,11 +509,11 @@
             shape_of(reaction.shape, f32),
             shape_of(reaction.shape, f32),
         ),
-        in_specs=[pl.BlockSpec(memory_space=pltpu.HBM)] * 8,
+        in_specs=[pl.BlockSpec(memory_space=pltpu.HBM)] * 7,
         out_specs=(pl.BlockSpec(memory_space=vmem),) * 3,
         scratch_shapes=[vmem(value.shape, value.dtype) for value in operands]
         + [
-            dma((8,)),
+            dma((7,)),
             vmem((3, 128, 128), f32),
             vmem((4, 128, 128), f32),
             vmem((2, 3, 16, 128), f32),
@@ -520,7 +528,7 @@
             vmem((4, 2, 1, 16, 128), f32),
             vmem((4, 2, 1, 8, 128), f32),
             vmem((4, 4, 8, 128), f32),
-            vmem((3, 8, 128), f32),
+            vmem((2, 8, 128), f32),
             vmem((trips, 8, 128), f32),
             dma((5, 8)),
             dma((5, 8)),

time: 54.7 us -> 54.9 us (level)
  Pallas kernels: 50.1 us -> 51.3 us
  local copies, waits for them, and re-layouts: 3.61 us -> 2.77 us
    pallas_call x1, Pallas kernels: 50.1 us -> 51.3 us  [per_device(): pl.pallas_call(functools.partial(kernel, sizes), out_shape=(shape_of(velo...]
    unnamed x7 -> x5, local copies, waits for them, and re-layouts: 3.61 us -> 2.77 us
where the time goes in v2:
time: 54.9 us; the launch traced here: 54.7 us
  Pallas kernels  51.3 us (93%)
  local copies, waits for them, and re-layouts  2.77 us (5%)
  between operations  0.65 us (1%)
    pallas_call x1, Pallas kernels, per_device(): pl.pallas_call(functools.partial(kernel, sizes), out_shape=(shape_of(velo...  51.3 us
    unnamed x5, local copies, waits for them, and re-layouts  2.77 us

profile of v2, /device:TPU:1, one launch (start us, length us, event | category | flops | bytes accessed | tf_op | source)
XLA Modules:
  0.0 54.7 jit_solution(3990525440905348451)
XLA Ops:
  0.6 0.0 copy-start
  0.6 0.8 %copy-done = f32[8,16,128]{2,1,0:T(8,128)S(1)} copy-done((f32[8,16,128]{2,1,0:T(8,128)S(1)}, f32[8,16,128]{2,1,0:T(8,128)}, u32[]{:S(2)}) %copy-start) | copy-done | bytes 65560
  1.5 51.3 %shard_map.94 = (f32[3,8,16,128]{3,2,1,0:T(8,128)S(1)}, f32[8,16,128]{2,1,0:T(8,128)S(1)}, f32[8,16,128]{2,1,0:T(8,128)S(1)}) custom-call(f32[3,8,16,128]{3,2,1,0:T(8,128)} %vel_hbm.1, f32[8,16,128]{2,1,0:T(8,128)S(1)} %copy-done, bf16[384,512]{1,0:T(8,128)(2,1)} %constant.10.clone.fine_z_hbm, bf16[496,432]{1,0:T(8,128)(2,1)} %constant.11.clone.fine_xy_hbm, ...), custom_call_target="tpu_custom_call" | custom-call | tf_op jit(solution)/shard_map/pallas_call | solution.py:505
  52.8 0.7 %copy.13 = f32[3,8,16,128]{3,2,1,0:T(8,128)} copy(f32[3,8,16,128]{3,2,1,0:T(8,128)S(1)} %get-tuple-element.6) | data formatting | bytes 393216
  53.5 0.6 %copy.14 = f32[8,16,128]{2,1,0:T(8,128)} copy(f32[8,16,128]{2,1,0:T(8,128)S(1)} %get-tuple-element.7) | data formatting | bytes 131072
  54.1 0.6 %copy.15 = f32[8,16,128]{2,1,0:T(8,128)} copy(f32[8,16,128]{2,1,0:T(8,128)S(1)} %get-tuple-element.8) | data formatting | bytes 131072
Async XLA Ops:
  0.6 0.8 %copy-start = (f32[8,16,128]{2,1,0:T(8,128)S(1)}, f32[8,16,128]{2,1,0:T(8,128)}, u32[]{:S(2)}) copy-start(f32[8,16,128]{2,1,0:T(8,128)} %rea_hbm.1) | copy-start | bytes 196612

commit v3 on v2

--- a/solution.py
+++ b/solution.py
@@ -214,6 +214,7 @@
     recv_sem,
     tree_send,
     tree_recv,
+    word,
 ):
     pairs = (
         (vel_hbm, vel_ref),
@@ -259,11 +260,34 @@
             for i, j in far_first(high_count, count_y // 2)
         ],
     )
-    partners = [at_side(side) for side in SIDES] + [who for stage in stages for who in stage]
+    def by_z(step):
+        return me_high * low_count + turn(me_low, step, low_count), me_y
+
+    def by_y(step):
+        return turn(me_high, step, high_count) * low_count + me_low, me_y
+
+    def by_pair(step):
+        return me_x, turn(me_pair, step, count_y // 2) * 2 + me_core
+
+    near = [by_z(1), by_z(-1), by_y(1), by_y(-1), by_pair(1), by_pair(-1)]
+    rounds = (
+        near[:4],
+        [by_z(2), by_z(-2), by_y(2), by_y(-2)],
+        [by_z(2), by_z(-2)] + near[4:],
+        near[4:] + [(me_x, me_pair * 2 + 1 - me_core)],
+    )
+    partners = [at_side(side) for side in SIDES] + near
 
     barrier = pltpu.get_barrier_semaphore()
     for who in partners:
         pl.semaphore_signal(barrier, inc=1, device_id=who, device_id_type=MESH)
+
+    def vouch(index):
+        for who in rounds[index]:
+            pl.semaphore_signal(word.at[index], inc=1, device_id=who, device_id_type=MESH)
+
+    def hear(index):
+        pl.semaphore_wait(word.at[index], len(rounds[index]))
 
     for load in loads[:3]:
         load.wait()
@@ -359,6 +383,7 @@
     three = (sx3, sy3, sc3, rx3, ry3, rc3)
     ones = [tuple(buf.at[k] for buf in (sx1, sy1, sc1, rx1, ry1, rc1)) for k in range(4)]
     copies = exchange(adv_q, None, three, 0, 3)
+    vouch(0)
     flights = list(copies)
 
     for load in loads[4:]:
@@ -400,15 +425,18 @@
         return plain_ref[6] * flat + plain_ref[2] * along + mass_term * value
 
     receive(adv_q, three, copies, 3)
+    hear(0)
     adv = []
     for c in range(3):
         adv.append(adv_q[c] * inverse_mass)
     ops_q[0] = 0.05 * divergence(adv, div_xy2, div_z2, plain_ref[6], plain_ref[2]) - base
     copies = exchange(ops_q.at[pl.ds(0, 1)], None, ones[0], 1, 1)
+    vouch(1)
     flights += copies
     for c in range(3):
         adv_ref[c] = adv[c].reshape(8, 16, 128)
     receive(ops_q.at[pl.ds(0, 1)], ones[0], copies, 1)
+    hear(1)
 
     def dot(first, second, scale):
         return jnp.sum(first * second * scale, axis=0, keepdims=True)
@@ -416,17 +444,21 @@
     z0 = ops_q[0]
     ops_q[1] = operate(z0)
     copies = exchange(ops_q.at[pl.ds(1, 1)], None, ones[1], 2, 1)
+    vouch(2)
     flights += copies
     part[0, 0:1, :] = dot(z0, z0, inverse_mult)
     part[0, 6:8, :] = jnp.zeros((2, 128), jnp.float32)
     receive(ops_q.at[pl.ds(1, 1)], ones[1], copies, 1)
+    hear(2)
     z1 = ops_q[1]
     ops_q[2] = operate(z1)
     copies = exchange(ops_q.at[pl.ds(2, 1)], None, ones[2], 3, 1)
+    vouch(3)
     flights += copies
     part[0, 1:2, :] = dot(z0, z1, inverse_mult)
     part[0, 2:3, :] = dot(z1, z1, inverse_mult)
     receive(ops_q.at[pl.ds(2, 1)], ones[2], copies, 1)
+    hear(3)
     z2 = ops_q[2]
     last = operate(z2)
     part[0, 3:4, :] = dot(z1, z2, inverse_mult)
@@ -495,6 +527,17 @@
         copy.wait_send()
 
 
+def store(*refs):
+    sources, targets, sems = refs[:3], refs[3:6], refs[6]
+    copies = [
+        pltpu.make_async_copy(a, b, sems.at[k]) for k, (a, b) in enumerate(zip(sources, targets))
+    ]
+    for copy in copies:
+        copy.start()
+    for copy in copies:
+        copy.wait()
+
+
 def per_device(sizes, velocity, reaction):
     consts = [jnp.asarray(value) for value in tables_for(reaction.shape[2])]
     operands = [velocity, reaction] + consts
@@ -502,7 +545,7 @@
     count_x, count_y, low_count = sizes
     trips = (2 * low_count - 1) + (count_x // low_count * count_y // 2 - 1)
     vmem, f32, dma = pltpu.VMEM, jnp.float32, pltpu.SemaphoreType.DMA
-    return pl.pallas_call(
+    results = pl.pallas_call(
         functools.partial(kernel, sizes),
         out_shape=(
             shape_of(velocity.shape, f32),
@@ -534,11 +577,20 @@
             dma((5, 8)),
             dma((trips,)),
             dma((trips,)),
+            pltpu.SemaphoreType.REGULAR((4,)),
         ],
         compiler_params=pltpu.CompilerParams(
             collective_id=0, has_side_effects=True, vmem_limit_bytes=54700 * 1024
         ),
     )(*operands)
+    return pl.pallas_call(
+        store,
+        out_shape=tuple(shape_of(value.shape, f32) for value in results),
+        in_specs=[pl.BlockSpec(memory_space=vmem)] * 3,
+        out_specs=(pl.BlockSpec(memory_space=pltpu.HBM),) * 3,
+        scratch_shapes=[dma((3,))],
+        compiler_params=pltpu.CompilerParams(vmem_limit_bytes=1024 * 1024),
+    )(*results)
 
 
 def solution(mesh):

time: 54.9 us -> 52.5 us (0.956)
  local copies, waits for them, and re-layouts: 2.77 us -> 0.83 us
    unnamed x5 -> x2, local copies, waits for them, and re-layouts: 2.77 us -> 0.83 us
    pallas_call x1, Pallas kernels: 51.3 us -> 50.1 us  [per_device(): pl.pallas_call(functools.partial(kernel, sizes), out_shape=(shape_of(velo...]
    pallas_call x0 -> x1, Pallas kernels: none -> 0.74 us  [per_device(): pl.pallas_call(store, out_shape=tuple((shape_of(value.shape, f32) for val...]
where the time goes in v3:
time: 52.5 us; the launch traced here: 52.3 us
  Pallas kernels  50.8 us (97%)
  local copies, waits for them, and re-layouts  0.83 us (2%)
  between operations  0.65 us (1%)
    pallas_call x1, Pallas kernels, per_device(): pl.pallas_call(functools.partial(kernel, sizes), out_shape=(shape_of(velo...  50.1 us

profile of v3, /device:TPU:1, one launch (start us, length us, event | category | flops | bytes accessed | tf_op | source)
XLA Modules:
  0.0 52.3 jit_solution(17958205020710594959)
XLA Ops:
  0.6 0.0 copy-start
  0.6 0.8 %copy-done = f32[8,16,128]{2,1,0:T(8,128)S(1)} copy-done((f32[8,16,128]{2,1,0:T(8,128)S(1)}, f32[8,16,128]{2,1,0:T(8,128)}, u32[]{:S(2)}) %copy-start) | copy-done | bytes 65560
  1.5 50.1 %shard_map.94 = (f32[3,8,16,128]{3,2,1,0:T(8,128)S(1)}, f32[8,16,128]{2,1,0:T(8,128)S(1)}, f32[8,16,128]{2,1,0:T(8,128)S(1)}) custom-call(f32[3,8,16,128]{3,2,1,0:T(8,128)} %vel_hbm.1, f32[8,16,128]{2,1,0:T(8,128)S(1)} %copy-done, bf16[384,512]{1,0:T(8,128)(2,1)} %constant.10.clone.fine_z_hbm, bf16[496,432]{1,0:T(8,128)(2,1)} %constant.11.clone.fine_xy_hbm, ...), custom_call_target="tpu_custom_call" | custom-call | tf_op jit(solution)/shard_map/pallas_call | solution.py:548
  51.6 0.7 %shard_map.95 = (f32[3,8,16,128]{3,2,1,0:T(8,128)}, f32[8,16,128]{2,1,0:T(8,128)}, f32[8,16,128]{2,1,0:T(8,128)}) custom-call(f32[3,8,16,128]{3,2,1,0:T(8,128)S(1)} %get-tuple-element.6.refs_0_, f32[8,16,128]{2,1,0:T(8,128)S(1)} %get-tuple-element.7.refs_1_, f32[8,16,128]{2,1,0:T(8,128)S(1)} %get-tuple-element.8.refs_2_), custom_call_target="tpu_custom_call" | custom-call | tf_op jit(solution)/shard_map/pallas_call | solution.py:586
Async XLA Ops:
  0.6 0.8 %copy-start = (f32[8,16,128]{2,1,0:T(8,128)S(1)}, f32[8,16,128]{2,1,0:T(8,128)}, u32[]{:S(2)}) copy-start(f32[8,16,128]{2,1,0:T(8,128)} %rea_hbm.1) | copy-start | bytes 196612

commit v4 on v3

--- a/solution.py
+++ b/solution.py
@@ -110,6 +110,10 @@
     back_xy = np.kron(back, back)
 
     op_xy = np.kron(stiff, np.diag(w_y2)) + np.kron(np.diag(w_x), sum_y @ np.kron(eye2, stiff))
+    for row in (0, 15):
+        pick = np.zeros((1, 16))
+        pick[0, row] = weights[0]
+        op_xy = np.concatenate([op_xy, np.kron(stiff, pick)], axis=0)
     op_z = np.kron(eye_z, stiff).T @ sum_z
     weak = np.diag(weights) @ deriv
     div_xy = np.concatenate(
@@ -134,14 +138,17 @@
             np.outer(np.kron(ones_x, half_y), half_z),
             np.outer(np.ones(128), w_z),
             np.outer(np.ones(128), w_z2),
+            np.outer(np.tile(np.concatenate([stiff[0], stiff[7]]), 8), ones_z),
+            np.outer(np.tile(w_x, 16), w_z2),
         ]
     ).astype(np.float32)
     from_right = np.concatenate(
         [right_factor(back_z), right_factor(op_z), right_factor(div_z), right_factor(div_z2)], axis=0
     )
-    from_left = np.concatenate(
-        [left_factor(op_xy), left_factor(div_xy), left_factor(div_xy2)], axis=1
-    )
+    from_left = np.zeros((144, 1920), ml_dtypes.bfloat16)
+    from_left[:, :384] = left_factor(op_xy)
+    from_left[:128, 384:1152] = left_factor(div_xy)
+    from_left[:128, 1152:] = left_factor(div_xy2)
     shapes_xy = np.zeros((496, 432), ml_dtypes.bfloat16)
     shapes_xy[:432, :192] = left_factor(fine_xy)
     shapes_xy[432:] = left_factor(back_xy)
@@ -215,6 +222,8 @@
     tree_send,
     tree_recv,
     word,
+    mass_q,
+    lines_q,
 ):
     pairs = (
         (vel_hbm, vel_ref),
@@ -230,6 +239,8 @@
         load.start()
 
     count_x, count_y, low_count = sizes
+    weights, deriv = spectral_tables()[:2]
+    corner_stiff = float((deriv.T @ np.diag(weights) @ deriv)[7, 7])
     high_count = count_x // low_count
     me_x, me_y = lax.axis_index("wide"), lax.axis_index("narrow")
     me_low, me_high = lax.rem(me_x, low_count), me_x // low_count
@@ -330,22 +341,31 @@
 
     has = {1: (me_x > 0, me_y > 0), -1: (me_x < count_x - 1, me_y < count_y - 1)}
 
-    def exchange(q_ref, slots, bufs, index, comps):
+    def exchange(q_ref, bufs, index, comps, only_x=False, ends=None, corners=0):
         sx, sy, sc, rx, ry, rc = bufs
         for c in range(comps):
             q = q_ref.at[c]
             sx[0, c] = q[112:128, :]
             sx[1, c] = q[0:16, :]
+            if only_x:
+                continue
             sy[0, c] = q[pl.ds(15, 8, stride=16), :]
             sy[1, c] = q[pl.ds(0, 8, stride=16), :]
             for k, row in enumerate((127, 112, 15, 0)):
                 sc[k, c : c + 1, :] = q[row : row + 1, :]
+        if ends is not None:
+            for k in range(2):
+                sy[k, comps] = ends[k]
+        for k in range(4 if corners else 0):
+            row = 0 if k >= 2 else 7
+            sc[k, comps : comps + 1, :] = ends[k % 2][row : row + 1, :]
         copies = []
-        for k, side in enumerate(SIDES):
+        for k, side in enumerate(SIDES[:2] if only_x else SIDES):
             if k < 2:
                 source, target = sx.at[k], rx.at[k]
             elif k < 4:
-                source, target = sy.at[k - 2], ry.at[k - 2]
+                lines = pl.ds(0, comps if ends is None else comps + 1)
+                source, target = sy.at[k - 2, lines], ry.at[k - 2, lines]
             else:
                 source, target = sc.at[k - 4], rc.at[k - 4]
             copies.append(
@@ -358,31 +378,38 @@
                     device_id_type=MESH,
                 )
             )
-        for copy in copies[4:] + copies[:4]:
+        copies = copies[:2] if only_x else copies[4:] + copies[:4]
+        for copy in copies:
             copy.start()
         return copies
 
     row_x = lax.broadcasted_iota(jnp.int32, (8, 128), 0)
 
-    def receive(q_ref, bufs, copies, comps):
-        sx, sy, sc, rx, ry, rc = bufs
+    def side_line(bufs, k, c):
+        ry, rc = bufs[4], bufs[5]
+        low = jnp.where(has[1][0], rc[k, c : c + 1, :], 0.0)
+        high = jnp.where(has[-1][0], rc[2 + k, c : c + 1, :], 0.0)
+        return ry[k, c] + jnp.where(row_x == 0, low, 0.0) + jnp.where(row_x == 7, high, 0.0)
+
+    ends_y = ((pl.ds(0, 8, stride=16), has[1][1]), (pl.ds(15, 8, stride=16), has[-1][1]))
+
+    def receive(q_ref, bufs, copies, comps, only_x=False):
+        rx = bufs[3]
         for copy in copies:
             copy.wait_recv()
         for c in range(comps):
             q = q_ref.at[c]
             q[0:16, :] = q[0:16, :] + jnp.where(has[1][0], rx[0, c], 0.0)
             q[112:128, :] = q[112:128, :] + jnp.where(has[-1][0], rx[1, c], 0.0)
-            for k, step in ((0, 1), (1, -1)):
-                line = ry[k, c]
-                low = jnp.where(has[1][0], rc[k, c : c + 1, :], 0.0)
-                high = jnp.where(has[-1][0], rc[2 + k, c : c + 1, :], 0.0)
-                line = line + jnp.where(row_x == 0, low, 0.0) + jnp.where(row_x == 7, high, 0.0)
-                rows = pl.ds(0 if step == 1 else 15, 8, stride=16)
-                q[rows, :] = q[rows, :] + jnp.where(has[step][1], line, 0.0)
+            if only_x:
+                continue
+            for k, (rows, there) in enumerate(ends_y):
+                line = side_line(bufs, k, c)
+                q[rows, :] = q[rows, :] + jnp.where(there, line, 0.0)
 
     three = (sx3, sy3, sc3, rx3, ry3, rc3)
     ones = [tuple(buf.at[k] for buf in (sx1, sy1, sc1, rx1, ry1, rc1)) for k in range(4)]
-    copies = exchange(adv_q, None, three, 0, 3)
+    copies = exchange(adv_q, three, 0, 3)
     vouch(0)
     flights = list(copies)
 
@@ -414,13 +441,13 @@
     op_z, div_z, div_z2 = (slice(back_rows + 384 * k, back_rows + 384 * k + 384) for k in range(3))
 
     def divergence(field, on_xy, on_z, scale_z, scale_xy):
-        flat = mul(left_ref[:, on_xy], stacked(jnp.concatenate(field[:2], axis=0)))
+        flat = mul(left_ref[:128, on_xy], stacked(jnp.concatenate(field[:2], axis=0)))
         return scale_z * flat + scale_xy * mul(joined(field[2]), right_ref[on_z, :])
 
     base = sum_yz(divergence(vel, div_xy, div_z, plain_ref[5], plain_ref[1]))
 
     def operate(value):
-        flat = mul(left_ref[:, op_xy], stacked(value))
+        flat = mul(left_ref[:128, op_xy], stacked(value))
         along = mul(joined(value), right_ref[op_z, :])
         return plain_ref[6] * flat + plain_ref[2] * along + mass_term * value
 
@@ -430,7 +457,14 @@
     for c in range(3):
         adv.append(adv_q[c] * inverse_mass)
     ops_q[0] = 0.05 * divergence(adv, div_xy2, div_z2, plain_ref[6], plain_ref[2]) - base
-    copies = exchange(ops_q.at[pl.ds(0, 1)], None, ones[0], 1, 1)
+    mass_q[...] = mass_term
+    copies = exchange(
+        ops_q.at[pl.ds(0, 1)],
+        ones[0],
+        1,
+        1,
+        ends=(mass_q[pl.ds(15, 8, stride=16), :], mass_q[pl.ds(0, 8, stride=16), :]),
+    )
     vouch(1)
     flights += copies
     for c in range(3):
@@ -442,22 +476,45 @@
         return jnp.sum(first * second * scale, axis=0, keepdims=True)
 
     z0 = ops_q[0]
-    ops_q[1] = operate(z0)
-    copies = exchange(ops_q.at[pl.ds(1, 1)], None, ones[1], 2, 1)
+    image = operate(z0)
+    ops_q[1] = image
+    lines_q[...] = jnp.sum((image * plain_ref[7]).reshape(16, 8, 128), axis=1)
+    copies = exchange(
+        ops_q.at[pl.ds(1, 1)],
+        ones[1],
+        2,
+        1,
+        ends=(lines_q[pl.ds(1, 8, stride=2), :], lines_q[pl.ds(0, 8, stride=2), :]),
+        corners=1,
+    )
     vouch(2)
     flights += copies
     part[0, 0:1, :] = dot(z0, z0, inverse_mult)
     part[0, 6:8, :] = jnp.zeros((2, 128), jnp.float32)
+    both = ((in_y == 0) & has[1][1]) | ((in_y == 15) & has[-1][1])
+    twice = plain_ref[2] * jnp.where(both, 2.0, 1.0)
+    for k, (rows_k, there) in enumerate(ends_y):
+        mass_q[rows_k, :] = mass_q[rows_k, :] + jnp.where(there, ones[0][4][k, 1], 0.0)
     receive(ops_q.at[pl.ds(1, 1)], ones[1], copies, 1)
     hear(2)
     z1 = ops_q[1]
-    ops_q[2] = operate(z1)
-    copies = exchange(ops_q.at[pl.ds(2, 1)], None, ones[2], 3, 1)
+    flat = mul(left_ref[:, op_xy], stacked(z1))
+    along = mul(joined(z1), right_ref[op_z, :])
+    extra = []
+    for k, (rows_k, there) in enumerate(ends_y):
+        own = ops_q[1, rows_k, :] - side_line(ones[1], k, 0)
+        line = side_line(ones[1], k, 1) + corner_stiff * own
+        share = plain_ref[6, 0:8, :] * flat[128 + 8 * k : 136 + 8 * k] + plain_ref[8, 0:8, :] * line
+        extra.append(jnp.where(there, share, 0.0))
+    ops_q[2] = plain_ref[6] * flat[:128] + twice * along + mass_q[...] * z1
+    for k, (rows_k, there) in enumerate(ends_y):
+        ops_q[2, rows_k, :] = ops_q[2, rows_k, :] + extra[k]
+    copies = exchange(ops_q.at[pl.ds(2, 1)], ones[2], 3, 1, only_x=True)
     vouch(3)
     flights += copies
     part[0, 1:2, :] = dot(z0, z1, inverse_mult)
     part[0, 2:3, :] = dot(z1, z1, inverse_mult)
-    receive(ops_q.at[pl.ds(2, 1)], ones[2], copies, 1)
+    receive(ops_q.at[pl.ds(2, 1)], ones[2], copies, 1, only_x=True)
     hear(3)
     z2 = ops_q[2]
     last = operate(z2)
@@ -483,7 +540,7 @@
             copy.start()
         if index == 0:
             ops_q[3] = last
-            copies = exchange(ops_q.at[pl.ds(3, 1)], None, ones[3], 4, 1)
+            copies = exchange(ops_q.at[pl.ds(3, 1)], ones[3], 4, 1)
             flights += copies
         for copy in copies_in:
             copy.wait_recv()
@@ -566,10 +623,10 @@
             vmem((2, 3, 8, 128), f32),
             vmem((4, 8, 128), f32),
             vmem((4, 2, 1, 16, 128), f32),
-            vmem((4, 2, 1, 8, 128), f32),
+            vmem((4, 2, 2, 8, 128), f32),
             vmem((4, 4, 8, 128), f32),
             vmem((4, 2, 1, 16, 128), f32),
-            vmem((4, 2, 1, 8, 128), f32),
+            vmem((4, 2, 2, 8, 128), f32),
             vmem((4, 4, 8, 128), f32),
             vmem((2, 8, 128), f32),
             vmem((trips, 8, 128), f32),
@@ -578,6 +635,8 @@
             dma((trips,)),
             dma((trips,)),
             pltpu.SemaphoreType.REGULAR((4,)),
+            vmem((128, 128), f32),
+            vmem((16, 128), f32),
         ],
         compiler_params=pltpu.CompilerParams(
             collective_id=0, has_side_effects=True, vmem_limit_bytes=54700 * 1024

time: 52.5 us -> 51.4 us (0.979)
  Pallas kernels: 50.8 us -> 49.7 us
    pallas_call x1, Pallas kernels: 50.1 us -> 49 us  [per_device(): pl.pallas_call(functools.partial(kernel, sizes), out_shape=(shape_of(velo...]
where the time goes in v4:
time: 51.4 us; the launch traced here: 51.2 us
  Pallas kernels  49.7 us (97%)
  local copies, waits for them, and re-layouts  0.83 us (2%)
  between operations  0.65 us (1%)
    pallas_call x1, Pallas kernels, per_device(): pl.pallas_call(functools.partial(kernel, sizes), out_shape=(shape_of(velo...  49 us

profile of v4, /device:TPU:1, one launch (start us, length us, event | category | flops | bytes accessed | tf_op | source)
XLA Modules:
  0.0 51.2 jit_solution(434629249407829849)
XLA Ops:
  0.6 0.0 copy-start
  0.6 0.8 %copy-done = f32[8,16,128]{2,1,0:T(8,128)S(1)} copy-done((f32[8,16,128]{2,1,0:T(8,128)S(1)}, f32[8,16,128]{2,1,0:T(8,128)}, u32[]{:S(2)}) %copy-start) | copy-done | bytes 65560
  1.5 49.0 %shard_map.94 = (f32[3,8,16,128]{3,2,1,0:T(8,128)S(1)}, f32[8,16,128]{2,1,0:T(8,128)S(1)}, f32[8,16,128]{2,1,0:T(8,128)S(1)}) custom-call(f32[3,8,16,128]{3,2,1,0:T(8,128)} %vel_hbm.1, f32[8,16,128]{2,1,0:T(8,128)S(1)} %copy-done, bf16[384,512]{1,0:T(8,128)(2,1)} %constant.10.clone.fine_z_hbm, bf16[496,432]{1,0:T(8,128)(2,1)} %constant.11.clone.fine_xy_hbm, ...), custom_call_target="tpu_custom_call" | custom-call | tf_op jit(solution)/shard_map/pallas_call | solution.py:605
  50.5 0.7 %shard_map.95 = (f32[3,8,16,128]{3,2,1,0:T(8,128)}, f32[8,16,128]{2,1,0:T(8,128)}, f32[8,16,128]{2,1,0:T(8,128)}) custom-call(f32[3,8,16,128]{3,2,1,0:T(8,128)S(1)} %get-tuple-element.6.refs_0_, f32[8,16,128]{2,1,0:T(8,128)S(1)} %get-tuple-element.7.refs_1_, f32[8,16,128]{2,1,0:T(8,128)S(1)} %get-tuple-element.8.refs_2_), custom_call_target="tpu_custom_call" | custom-call | tf_op jit(solution)/shard_map/pallas_call | solution.py:645
Async XLA Ops:
  0.6 0.8 %copy-start = (f32[8,16,128]{2,1,0:T(8,128)S(1)}, f32[8,16,128]{2,1,0:T(8,128)}, u32[]{:S(2)}) copy-start(f32[8,16,128]{2,1,0:T(8,128)} %rea_hbm.1) | copy-start | bytes 196612

commit v5 on v3

--- a/solution.py
+++ b/solution.py
@@ -12,6 +12,7 @@
 MESH = pl.DeviceIdType.MESH
 SHIFT = 4.0
 SIDES = ((1, 0), (-1, 0), (0, 1), (0, -1), (1, 1), (1, -1), (-1, 1), (-1, -1))
+FAR = ((2, 0), (-2, 0), (2, 1), (2, -1), (-2, 1), (-2, -1))
 
 
 def legendre_pair(order, nodes):
@@ -110,6 +111,9 @@
     back_xy = np.kron(back, back)
 
     op_xy = np.kron(stiff, np.diag(w_y2)) + np.kron(np.diag(w_x), sum_y @ np.kron(eye2, stiff))
+    op_apart = np.concatenate(
+        [np.kron(stiff, np.eye(16)), np.kron(np.eye(8), sum_y @ np.kron(eye2, stiff))], axis=0
+    )
     op_z = np.kron(eye_z, stiff).T @ sum_z
     weak = np.diag(weights) @ deriv
     div_xy = np.concatenate(
@@ -134,14 +138,19 @@
             np.outer(np.kron(ones_x, half_y), half_z),
             np.outer(np.ones(128), w_z),
             np.outer(np.ones(128), w_z2),
+            np.outer(np.tile(np.concatenate([stiff[0], stiff[7]]), 8), ones_z),
+            np.outer(np.kron(w_x, np.ones(16)), w_z2),
+            np.outer(np.kron(ones_x, w_y2), w_z2),
         ]
     ).astype(np.float32)
     from_right = np.concatenate(
         [right_factor(back_z), right_factor(op_z), right_factor(div_z), right_factor(div_z2)], axis=0
     )
-    from_left = np.concatenate(
-        [left_factor(op_xy), left_factor(div_xy), left_factor(div_xy2)], axis=1
-    )
+    from_left = np.zeros((256, 2304), ml_dtypes.bfloat16)
+    from_left[:128, :384] = left_factor(op_xy)
+    from_left[:128, 384:1152] = left_factor(div_xy)
+    from_left[:128, 1152:1920] = left_factor(div_xy2)
+    from_left[:, 1920:] = left_factor(op_apart)
     shapes_xy = np.zeros((496, 432), ml_dtypes.bfloat16)
     shapes_xy[:432, :192] = left_factor(fine_xy)
     shapes_xy[432:] = left_factor(back_xy)
@@ -215,6 +224,13 @@
     tree_send,
     tree_recv,
     word,
+    mass_q,
+    local_mass,
+    lines_q,
+    sums_x,
+    sums_y,
+    far_x,
+    far_c,
 ):
     pairs = (
         (vel_hbm, vel_ref),
@@ -230,6 +246,8 @@
         load.start()
 
     count_x, count_y, low_count = sizes
+    weights, deriv = spectral_tables()[:2]
+    stiff = [[float(v) for v in row] for row in deriv.T @ np.diag(weights) @ deriv]
     high_count = count_x // low_count
     me_x, me_y = lax.axis_index("wide"), lax.axis_index("narrow")
     me_low, me_high = lax.rem(me_x, low_count), me_x // low_count
@@ -330,59 +348,78 @@
 
     has = {1: (me_x > 0, me_y > 0), -1: (me_x < count_x - 1, me_y < count_y - 1)}
 
-    def exchange(q_ref, slots, bufs, index, comps):
+    def pack(q, bufs, c):
+        sx, sy, sc = bufs[:3]
+        sx[0, c] = q[112:128, :]
+        sx[1, c] = q[0:16, :]
+        sy[0, c] = q[pl.ds(15, 8, stride=16), :]
+        sy[1, c] = q[pl.ds(0, 8, stride=16), :]
+        for k, row in enumerate((127, 112, 15, 0)):
+            sc[k, c : c + 1, :] = q[row : row + 1, :]
+
+    def launch(bufs, index, comps, far=False):
         sx, sy, sc, rx, ry, rc = bufs
-        for c in range(comps):
-            q = q_ref.at[c]
-            sx[0, c] = q[112:128, :]
-            sx[1, c] = q[0:16, :]
-            sy[0, c] = q[pl.ds(15, 8, stride=16), :]
-            sy[1, c] = q[pl.ds(0, 8, stride=16), :]
-            for k, row in enumerate((127, 112, 15, 0)):
-                sc[k, c : c + 1, :] = q[row : row + 1, :]
+        used = pl.ds(0, comps)
+        moves = []
+        for k in range(4):
+            moves.append((SIDES[4 + k], sc.at[k], rc.at[k]))
+        if far:
+            for k in range(4):
+                moves.append((FAR[2 + k], sc.at[k], far_c.at[k]))
+            for k in range(2):
+                moves.append((FAR[k], sx.at[k, 0], far_x.at[k]))
+        for k in range(2):
+            moves.append((SIDES[k], sx.at[k, used], rx.at[k, used]))
+        for k in range(2):
+            moves.append((SIDES[2 + k], sy.at[k, used], ry.at[k, used]))
         copies = []
-        for k, side in enumerate(SIDES):
-            if k < 2:
-                source, target = sx.at[k], rx.at[k]
-            elif k < 4:
-                source, target = sy.at[k - 2], ry.at[k - 2]
-            else:
-                source, target = sc.at[k - 4], rc.at[k - 4]
-            copies.append(
-                pltpu.make_async_remote_copy(
-                    src_ref=source,
-                    dst_ref=target,
-                    send_sem=send_sem.at[index, k],
-                    recv_sem=recv_sem.at[index, k],
-                    device_id=at_side(side),
-                    device_id_type=MESH,
-                )
+        for k, (side, source, target) in enumerate(moves):
+            copy = pltpu.make_async_remote_copy(
+                src_ref=source,
+                dst_ref=target,
+                send_sem=send_sem.at[index, k],
+                recv_sem=recv_sem.at[index, k],
+                device_id=at_side(side),
+                device_id_type=MESH,
             )
-        for copy in copies[4:] + copies[:4]:
             copy.start()
+            copies.append(copy)
         return copies
 
     row_x = lax.broadcasted_iota(jnp.int32, (8, 128), 0)
 
-    def receive(q_ref, bufs, copies, comps):
-        sx, sy, sc, rx, ry, rc = bufs
+    def side_line(bufs, k, c):
+        ry, rc = bufs[4], bufs[5]
+        low = jnp.where(has[1][0], rc[k, c : c + 1, :], 0.0)
+        high = jnp.where(has[-1][0], rc[2 + k, c : c + 1, :], 0.0)
+        return ry[k, c] + jnp.where(row_x == 0, low, 0.0) + jnp.where(row_x == 7, high, 0.0)
+
+    ends_y = ((pl.ds(0, 8, stride=16), has[1][1]), (pl.ds(15, 8, stride=16), has[-1][1]))
+
+    row_y = lax.broadcasted_iota(jnp.int32, (16, 128), 0)
+
+    def side_face(face, corner, k, row):
+        low = jnp.where(has[1][1], corner[2 * k, row : row + 1, :], 0.0)
+        high = jnp.where(has[-1][1], corner[2 * k + 1, row : row + 1, :], 0.0)
+        return face + jnp.where(row_y == 0, low, 0.0) + jnp.where(row_y == 15, high, 0.0)
+
+    ends_x = ((slice(0, 16), has[1][0]), (slice(112, 128), has[-1][0]))
+
+    def receive(fields, bufs, copies):
+        rx = bufs[3]
         for copy in copies:
             copy.wait_recv()
-        for c in range(comps):
-            q = q_ref.at[c]
-            q[0:16, :] = q[0:16, :] + jnp.where(has[1][0], rx[0, c], 0.0)
-            q[112:128, :] = q[112:128, :] + jnp.where(has[-1][0], rx[1, c], 0.0)
-            for k, step in ((0, 1), (1, -1)):
-                line = ry[k, c]
-                low = jnp.where(has[1][0], rc[k, c : c + 1, :], 0.0)
-                high = jnp.where(has[-1][0], rc[2 + k, c : c + 1, :], 0.0)
-                line = line + jnp.where(row_x == 0, low, 0.0) + jnp.where(row_x == 7, high, 0.0)
-                rows = pl.ds(0 if step == 1 else 15, 8, stride=16)
-                q[rows, :] = q[rows, :] + jnp.where(has[step][1], line, 0.0)
+        for c, q in enumerate(fields):
+            for k, (rows, there) in enumerate(ends_x):
+                q[rows, :] = q[rows, :] + jnp.where(there, rx[k, c], 0.0)
+            for k, (rows, there) in enumerate(ends_y):
+                q[rows, :] = q[rows, :] + jnp.where(there, side_line(bufs, k, c), 0.0)
 
     three = (sx3, sy3, sc3, rx3, ry3, rc3)
-    ones = [tuple(buf.at[k] for buf in (sx1, sy1, sc1, rx1, ry1, rc1)) for k in range(4)]
-    copies = exchange(adv_q, None, three, 0, 3)
+    ones = [tuple(buf.at[k] for buf in (sx1, sy1, sc1, rx1, ry1, rc1)) for k in range(3)]
+    for c in range(3):
+        pack(adv_q.at[c], three, c)
+    copies = launch(three, 0, 3)
     vouch(0)
     flights = list(copies)
 
@@ -395,6 +432,10 @@
     cross_x = ((in_x == 0) & has[1][0]) | ((in_x == 7) & has[-1][0])
     cross_y = ((in_y == 0) & has[1][1]) | ((in_y == 15) & has[-1][1])
     cross = jnp.where(cross_x, 0.5, 1.0) * jnp.where(cross_y, 0.5, 1.0)
+    twice_x, twice_y = jnp.where(cross_x, 2.0, 1.0), jnp.where(cross_y, 2.0, 1.0)
+    scale_y = plain_ref[8] * twice_x
+    scale_x = plain_ref[9] * twice_y
+    scale_z = plain_ref[2] * twice_x * twice_y
     local_half = plain_ref[4]
     inverse_mult = cross * local_half
     inverse_mass = plain_ref[3] * cross
@@ -408,58 +449,89 @@
         down = pltpu.roll(value, 127, 0)
         return value + jnp.where(in_y == 8, up, 0.0) + jnp.where(in_y == 7, down, 0.0)
 
-    mass_term = sum_yz(plain_ref[0] * rea_ref[...].reshape(128, 128)) - SHIFT * cross
+    mass_q[...] = sum_yz(plain_ref[0] * rea_ref[...].reshape(128, 128)) - SHIFT * cross
     vel = [vel_ref[c].reshape(128, 128) for c in range(3)]
+    local_mass[...] = mass_q[...]
     op_xy, div_xy, div_xy2 = (slice(0, 384), slice(384, 1152), slice(1152, 1920))
+    op_apart = slice(1920, 2304)
     op_z, div_z, div_z2 = (slice(back_rows + 384 * k, back_rows + 384 * k + 384) for k in range(3))
 
     def divergence(field, on_xy, on_z, scale_z, scale_xy):
-        flat = mul(left_ref[:, on_xy], stacked(jnp.concatenate(field[:2], axis=0)))
+        flat = mul(left_ref[:128, on_xy], stacked(jnp.concatenate(field[:2], axis=0)))
         return scale_z * flat + scale_xy * mul(joined(field[2]), right_ref[on_z, :])
 
     base = sum_yz(divergence(vel, div_xy, div_z, plain_ref[5], plain_ref[1]))
 
     def operate(value):
-        flat = mul(left_ref[:, op_xy], stacked(value))
+        flat = mul(left_ref[:128, op_xy], stacked(value))
         along = mul(joined(value), right_ref[op_z, :])
-        return plain_ref[6] * flat + plain_ref[2] * along + mass_term * value
-
-    receive(adv_q, three, copies, 3)
+        return plain_ref[6] * flat + plain_ref[2] * along + local_mass[...] * value
+
     hear(0)
+    vouch(1)
+    receive([adv_q.at[c] for c in range(3)], three, copies)
     adv = []
     for c in range(3):
         adv.append(adv_q[c] * inverse_mass)
     ops_q[0] = 0.05 * divergence(adv, div_xy2, div_z2, plain_ref[6], plain_ref[2]) - base
-    copies = exchange(ops_q.at[pl.ds(0, 1)], None, ones[0], 1, 1)
-    vouch(1)
+    pack(ops_q.at[0], ones[0], 0)
+    pack(mass_q, ones[0], 1)
+    copies = launch(ones[0], 1, 2)
     flights += copies
+    hear(1)
+    vouch(2)
     for c in range(3):
         adv_ref[c] = adv[c].reshape(8, 16, 128)
-    receive(ops_q.at[pl.ds(0, 1)], ones[0], copies, 1)
-    hear(1)
+    receive([ops_q.at[0], mass_q], ones[0], copies)
+    hear(2)
 
     def dot(first, second, scale):
         return jnp.sum(first * second * scale, axis=0, keepdims=True)
 
     z0 = ops_q[0]
-    ops_q[1] = operate(z0)
-    copies = exchange(ops_q.at[pl.ds(1, 1)], None, ones[1], 2, 1)
-    vouch(2)
+    image = operate(z0)
+    ops_q[1] = image
+    pack(ops_q.at[1], ones[1], 0)
+    sx, sy, sc = ones[1][:3]
+    lines_q[...] = jnp.sum((image * plain_ref[7]).reshape(16, 8, 128), axis=1)
+    for k, end in ((0, 7), (1, 0)):
+        face = stiff[end][0] * image[0:16]
+        for i in range(1, 8):
+            face = face + stiff[end][i] * image[16 * i : 16 * i + 16]
+        sx[k, 1] = face
+        sc[2 * k, 2:3, :] = face[15:16]
+        sc[2 * k + 1, 2:3, :] = face[0:1]
+        line = lines_q[pl.ds(1 - k, 8, stride=2), :]
+        sy[k, 1] = line
+        sc[k, 1:2, :] = line[7:8]
+        sc[2 + k, 1:2, :] = line[0:1]
+    copies = launch(ones[1], 2, 2, far=True)
     flights += copies
+    vouch(3)
     part[0, 0:1, :] = dot(z0, z0, inverse_mult)
     part[0, 6:8, :] = jnp.zeros((2, 128), jnp.float32)
-    receive(ops_q.at[pl.ds(1, 1)], ones[1], copies, 1)
-    hear(2)
+    receive([ops_q.at[1]], ones[1], copies)
+    hear(3)
     z1 = ops_q[1]
-    ops_q[2] = operate(z1)
-    copies = exchange(ops_q.at[pl.ds(2, 1)], None, ones[2], 3, 1)
-    vouch(3)
-    flights += copies
+    rx, ry, rc = ones[1][3:]
+    apart = mul(left_ref[:, op_apart], stacked(z1))
+    along = mul(joined(z1), right_ref[op_z, :])
+    sums_x[...] = apart[:128]
+    sums_y[...] = apart[128:]
+    two = (me_x > 1, me_x < count_x - 2)
+    for k, (rows_k, there) in enumerate(ends_x):
+        mine = ops_q[1, rows_k, :] - side_face(rx[k, 0], rc, k, 0)
+        other = jnp.where(two[k], side_face(far_x[k], far_c, k, 0), 0.0)
+        face = side_face(rx[k, 1], rc, k, 2) + stiff[7][7] * mine + stiff[7][0] * other
+        sums_x[rows_k, :] = sums_x[rows_k, :] + jnp.where(there, face, 0.0)
+    for k, (rows_k, there) in enumerate(ends_y):
+        mine = ops_q[1, rows_k, :] - side_line(ones[1], k, 0)
+        line = side_line(ones[1], k, 1) + stiff[7][7] * mine
+        sums_y[rows_k, :] = sums_y[rows_k, :] + jnp.where(there, line, 0.0)
+    z2 = scale_x * sums_x[...] + scale_y * sums_y[...] + scale_z * along + mass_q[...] * z1
+    ops_q[2] = z2
     part[0, 1:2, :] = dot(z0, z1, inverse_mult)
     part[0, 2:3, :] = dot(z1, z1, inverse_mult)
-    receive(ops_q.at[pl.ds(2, 1)], ones[2], copies, 1)
-    hear(3)
-    z2 = ops_q[2]
     last = operate(z2)
     part[0, 3:4, :] = dot(z1, z2, inverse_mult)
     part[0, 4:5, :] = dot(z2, z2, inverse_mult)
@@ -483,7 +555,8 @@
             copy.start()
         if index == 0:
             ops_q[3] = last
-            copies = exchange(ops_q.at[pl.ds(3, 1)], None, ones[3], 4, 1)
+            pack(ops_q.at[3], ones[2], 0)
+            copies = launch(ones[2], 3, 1)
             flights += copies
         for copy in copies_in:
             copy.wait_recv()
@@ -495,7 +568,7 @@
         flights += copies_in
         slot += len(stage)
 
-    receive(ops_q.at[pl.ds(3, 1)], ones[3], copies, 1)
+    receive([ops_q.at[3]], ones[2], copies)
     sums = jnp.broadcast_to(jnp.sum(total, axis=1, keepdims=True), (8, 128))
     g00, g01, g11, g12, g22, g23 = (sums[k : k + 1, :] for k in range(6))
     h00 = g01 + SHIFT * g00
@@ -565,19 +638,26 @@
             vmem((2, 3, 16, 128), f32),
             vmem((2, 3, 8, 128), f32),
             vmem((4, 8, 128), f32),
-            vmem((4, 2, 1, 16, 128), f32),
-            vmem((4, 2, 1, 8, 128), f32),
-            vmem((4, 4, 8, 128), f32),
-            vmem((4, 2, 1, 16, 128), f32),
-            vmem((4, 2, 1, 8, 128), f32),
-            vmem((4, 4, 8, 128), f32),
+            vmem((3, 2, 2, 16, 128), f32),
+            vmem((3, 2, 2, 8, 128), f32),
+            vmem((3, 4, 8, 128), f32),
+            vmem((3, 2, 2, 16, 128), f32),
+            vmem((3, 2, 2, 8, 128), f32),
+            vmem((3, 4, 8, 128), f32),
             vmem((2, 8, 128), f32),
             vmem((trips, 8, 128), f32),
-            dma((5, 8)),
-            dma((5, 8)),
+            dma((4, 14)),
+            dma((4, 14)),
             dma((trips,)),
             dma((trips,)),
             pltpu.SemaphoreType.REGULAR((4,)),
+            vmem((128, 128), f32),
+            vmem((128, 128), f32),
+            vmem((16, 128), f32),
+            vmem((128, 128), f32),
+            vmem((128, 128), f32),
+            vmem((2, 16, 128), f32),
+            vmem((4, 8, 128), f32),
         ],
         compiler_params=pltpu.CompilerParams(
             collective_id=0, has_side_effects=True, vmem_limit_bytes=54700 * 1024

time: 52.5 us -> 49.5 us (0.943)
  Pallas kernels: 50.8 us -> 47.8 us
    pallas_call x1, Pallas kernels: 50.1 us -> 47.1 us  [per_device(): pl.pallas_call(functools.partial(kernel, sizes), out_shape=(shape_of(velo...]
where the time goes in v5:
time: 49.5 us; the launch traced here: 49.3 us
  Pallas kernels  47.8 us (97%)
  local copies, waits for them, and re-layouts  0.83 us (2%)
  between operations  0.65 us (1%)
    pallas_call x1, Pallas kernels, per_device(): pl.pallas_call(functools.partial(kernel, sizes), out_shape=(shape_of(velo...  47.1 us

profile of v5, /device:TPU:1, one launch (start us, length us, event | category | flops | bytes accessed | tf_op | source)
XLA Modules:
  0.0 49.3 jit_solution(2433797195821253779)
XLA Ops:
  0.6 0.0 copy-start
  0.6 0.8 %copy-done = f32[8,16,128]{2,1,0:T(8,128)S(1)} copy-done((f32[8,16,128]{2,1,0:T(8,128)S(1)}, f32[8,16,128]{2,1,0:T(8,128)}, u32[]{:S(2)}) %copy-start) | copy-done | bytes 65560
  1.5 47.1 %shard_map.94 = (f32[3,8,16,128]{3,2,1,0:T(8,128)S(1)}, f32[8,16,128]{2,1,0:T(8,128)S(1)}, f32[8,16,128]{2,1,0:T(8,128)S(1)}) custom-call(f32[3,8,16,128]{3,2,1,0:T(8,128)} %vel_hbm.1, f32[8,16,128]{2,1,0:T(8,128)S(1)} %copy-done, bf16[384,512]{1,0:T(8,128)(2,1)} %constant.10.clone.fine_z_hbm, bf16[496,432]{1,0:T(8,128)(2,1)} %constant.11.clone.fine_xy_hbm, ...), custom_call_target="tpu_custom_call" | custom-call | tf_op jit(solution)/shard_map/pallas_call | solution.py:621
  48.6 0.7 %shard_map.95 = (f32[3,8,16,128]{3,2,1,0:T(8,128)}, f32[8,16,128]{2,1,0:T(8,128)}, f32[8,16,128]{2,1,0:T(8,128)}) custom-call(f32[3,8,16,128]{3,2,1,0:T(8,128)S(1)} %get-tuple-element.6.refs_0_, f32[8,16,128]{2,1,0:T(8,128)S(1)} %get-tuple-element.7.refs_1_, f32[8,16,128]{2,1,0:T(8,128)S(1)} %get-tuple-element.8.refs_2_), custom_call_target="tpu_custom_call" | custom-call | tf_op jit(solution)/shard_map/pallas_call | solution.py:666
Async XLA Ops:
  0.6 0.8 %copy-start = (f32[8,16,128]{2,1,0:T(8,128)S(1)}, f32[8,16,128]{2,1,0:T(8,128)}, u32[]{:S(2)}) copy-start(f32[8,16,128]{2,1,0:T(8,128)} %rea_hbm.1) | copy-start | bytes 196612

commit v6 on v5

--- a/solution.py
+++ b/solution.py
@@ -119,9 +119,8 @@
     div_xy = np.concatenate(
         [np.kron(weak, np.diag(w_y)), np.kron(np.diag(w_x), np.kron(eye2, weak))], axis=1
     )
-    div_xy2 = np.concatenate(
-        [np.kron(weak, np.diag(w_y2)), np.kron(np.diag(w_x), sum_y @ np.kron(eye2, weak))], axis=1
-    )
+    div_x = np.kron(weak, np.eye(16))
+    div_y = np.kron(np.eye(8), sum_y @ np.kron(eye2, weak))
     div_z = np.kron(eye_z, weak).T
     div_z2 = div_z @ sum_z
 
@@ -141,6 +140,7 @@
             np.outer(np.tile(np.concatenate([stiff[0], stiff[7]]), 8), ones_z),
             np.outer(np.kron(w_x, np.ones(16)), w_z2),
             np.outer(np.kron(ones_x, w_y2), w_z2),
+            np.outer(np.tile(np.concatenate([weak[0], weak[7]]), 8) / np.kron(ones_x, w_y2), ones_z),
         ]
     ).astype(np.float32)
     from_right = np.concatenate(
@@ -149,7 +149,8 @@
     from_left = np.zeros((256, 2304), ml_dtypes.bfloat16)
     from_left[:128, :384] = left_factor(op_xy)
     from_left[:128, 384:1152] = left_factor(div_xy)
-    from_left[:128, 1152:1920] = left_factor(div_xy2)
+    from_left[:128, 1152:1536] = left_factor(div_x)
+    from_left[:128, 1536:1920] = left_factor(div_y)
     from_left[:, 1920:] = left_factor(op_apart)
     shapes_xy = np.zeros((496, 432), ml_dtypes.bfloat16)
     shapes_xy[:432, :192] = left_factor(fine_xy)
@@ -231,6 +232,7 @@
     sums_y,
     far_x,
     far_c,
+    inverse_q,
 ):
     pairs = (
         (vel_hbm, vel_ref),
@@ -248,6 +250,8 @@
     count_x, count_y, low_count = sizes
     weights, deriv = spectral_tables()[:2]
     stiff = [[float(v) for v in row] for row in deriv.T @ np.diag(weights) @ deriv]
+    slope = [[float(v) for v in row] for row in np.diag(weights) @ deriv @ np.diag(1.0 / weights)]
+    thick = float(2.0 * weights[0])
     high_count = count_x // low_count
     me_x, me_y = lax.axis_index("wide"), lax.axis_index("narrow")
     me_low, me_high = lax.rem(me_x, low_count), me_x // low_count
@@ -294,7 +298,7 @@
         [by_z(2), by_z(-2)] + near[4:],
         near[4:] + [(me_x, me_pair * 2 + 1 - me_core)],
     )
-    partners = [at_side(side) for side in SIDES] + near
+    partners = [at_side(side) for side in SIDES + FAR] + near
 
     barrier = pltpu.get_barrier_semaphore()
     for who in partners:
@@ -347,6 +351,20 @@
     pl.semaphore_wait(barrier, len(partners))
 
     has = {1: (me_x > 0, me_y > 0), -1: (me_x < count_x - 1, me_y < count_y - 1)}
+    for load in loads[4:]:
+        load.wait()
+
+    rows = lax.broadcasted_iota(jnp.int32, (128, 128), 0)
+    in_x, in_y = rows // 16, lax.rem(rows, 16)
+    lane = lax.broadcasted_iota(jnp.int32, (128, 128), 1)
+    in_z = lax.rem(lane, 8)
+    cross_x = ((in_x == 0) & has[1][0]) | ((in_x == 7) & has[-1][0])
+    cross_y = ((in_y == 0) & has[1][1]) | ((in_y == 15) & has[-1][1])
+    cross = jnp.where(cross_x, 0.5, 1.0) * jnp.where(cross_y, 0.5, 1.0)
+    twice_x, twice_y = jnp.where(cross_x, 2.0, 1.0), jnp.where(cross_y, 2.0, 1.0)
+    scale_y = plain_ref[8] * twice_x
+    scale_x = plain_ref[9] * twice_y
+    scale_z = plain_ref[2] * twice_x * twice_y
 
     def pack(q, bufs, c):
         sx, sy, sc = bufs[:3]
@@ -357,17 +375,27 @@
         for k, row in enumerate((127, 112, 15, 0)):
             sc[k, c : c + 1, :] = q[row : row + 1, :]
 
-    def launch(bufs, index, comps, far=False):
+    def attach(bufs, c, k, face):
+        sx, sy, sc = bufs[:3]
+        sx[k, c] = face
+        sc[2 * k, c + 1 : c + 2, :] = face[15:16]
+        sc[2 * k + 1, c + 1 : c + 2, :] = face[0:1]
+        line = lines_q[pl.ds(1 - k, 8, stride=2), :]
+        sy[k, c] = line
+        sc[k, c : c + 1, :] = line[7:8]
+        sc[2 + k, c : c + 1, :] = line[0:1]
+
+    def launch(bufs, index, comps, far=None):
         sx, sy, sc, rx, ry, rc = bufs
         used = pl.ds(0, comps)
         moves = []
         for k in range(4):
             moves.append((SIDES[4 + k], sc.at[k], rc.at[k]))
-        if far:
+        if far is not None:
             for k in range(4):
-                moves.append((FAR[2 + k], sc.at[k], far_c.at[k]))
+                moves.append((FAR[2 + k], sc.at[k], far_c.at[far, k]))
             for k in range(2):
-                moves.append((FAR[k], sx.at[k, 0], far_x.at[k]))
+                moves.append((FAR[k], sx.at[k, 0], far_x.at[far, k]))
         for k in range(2):
             moves.append((SIDES[k], sx.at[k, used], rx.at[k, used]))
         for k in range(2):
@@ -419,23 +447,20 @@
     ones = [tuple(buf.at[k] for buf in (sx1, sy1, sc1, rx1, ry1, rc1)) for k in range(3)]
     for c in range(3):
         pack(adv_q.at[c], three, c)
-    copies = launch(three, 0, 3)
+    lines_q[...] = jnp.sum(
+        (adv_q[1] * plain_ref[10] * jnp.where(cross_y, 0.5, 1.0)).reshape(16, 8, 128), axis=1
+    )
+    outer = (jnp.where(has[1][0], 0.5, 1.0), jnp.where(has[-1][0], 0.5, 1.0))
+    for k, end in ((0, 7), (1, 0)):
+        face = (slope[end][0] * outer[0]) * adv_q[0, 0:16, :]
+        face = face + (slope[end][7] * outer[1]) * adv_q[0, 112:128, :]
+        for i in range(1, 7):
+            face = face + slope[end][i] * adv_q[0, 16 * i : 16 * i + 16, :]
+        attach(three, 3, k, face)
+    copies = launch(three, 0, 4, far=0)
     vouch(0)
     flights = list(copies)
 
-    for load in loads[4:]:
-        load.wait()
-    rows = lax.broadcasted_iota(jnp.int32, (128, 128), 0)
-    in_x, in_y = rows // 16, lax.rem(rows, 16)
-    lane = lax.broadcasted_iota(jnp.int32, (128, 128), 1)
-    in_z = lax.rem(lane, 8)
-    cross_x = ((in_x == 0) & has[1][0]) | ((in_x == 7) & has[-1][0])
-    cross_y = ((in_y == 0) & has[1][1]) | ((in_y == 15) & has[-1][1])
-    cross = jnp.where(cross_x, 0.5, 1.0) * jnp.where(cross_y, 0.5, 1.0)
-    twice_x, twice_y = jnp.where(cross_x, 2.0, 1.0), jnp.where(cross_y, 2.0, 1.0)
-    scale_y = plain_ref[8] * twice_x
-    scale_x = plain_ref[9] * twice_y
-    scale_z = plain_ref[2] * twice_x * twice_y
     local_half = plain_ref[4]
     inverse_mult = cross * local_half
     inverse_mass = plain_ref[3] * cross
@@ -452,7 +477,8 @@
     mass_q[...] = sum_yz(plain_ref[0] * rea_ref[...].reshape(128, 128)) - SHIFT * cross
     vel = [vel_ref[c].reshape(128, 128) for c in range(3)]
     local_mass[...] = mass_q[...]
-    op_xy, div_xy, div_xy2 = (slice(0, 384), slice(384, 1152), slice(1152, 1920))
+    op_xy, div_xy = slice(0, 384), slice(384, 1152)
+    div_x, div_y = slice(1152, 1536), slice(1536, 1920)
     op_apart = slice(1920, 2304)
     op_z, div_z, div_z2 = (slice(back_rows + 384 * k, back_rows + 384 * k + 384) for k in range(3))
 
@@ -467,47 +493,61 @@
         along = mul(joined(value), right_ref[op_z, :])
         return plain_ref[6] * flat + plain_ref[2] * along + local_mass[...] * value
 
+    ops_q[0] = base
+    pack(ops_q.at[0], ones[0], 0)
+    pack(mass_q, ones[0], 1)
+    later = launch(ones[0], 1, 2)
+    flights += later
     hear(0)
     vouch(1)
+    inverse_q[...] = inverse_mass
+    two = (me_x > 1, me_x < count_x - 2)
     receive([adv_q.at[c] for c in range(3)], three, copies)
     adv = []
     for c in range(3):
         adv.append(adv_q[c] * inverse_mass)
-    ops_q[0] = 0.05 * divergence(adv, div_xy2, div_z2, plain_ref[6], plain_ref[2]) - base
-    pack(ops_q.at[0], ones[0], 0)
-    pack(mass_q, ones[0], 1)
-    copies = launch(ones[0], 1, 2)
-    flights += copies
+    sums_x[...] = mul(left_ref[:128, div_x], stacked(adv[0]))
+    sums_y[...] = mul(left_ref[:128, div_y], stacked(adv[1]))
+    along = mul(joined(adv[2]), right_ref[div_z2, :])
+    rx, ry, rc = three[3:]
+    for k, (rows_k, there) in enumerate(ends_x):
+        near_end, far_end = 7 - 7 * k, 7 * k
+        mine = adv_q[0, rows_k, :] - side_face(rx[k, 0], rc, k, 0)
+        other = jnp.where(two[k], side_face(far_x[0, k], far_c[0], k, 0), 0.0)
+        face = side_face(rx[k, 3], rc, k, 4)
+        face = face + (0.5 * slope[near_end][near_end]) * mine
+        face = face + (0.5 * slope[near_end][far_end]) * other
+        face = face * (thick * inverse_q[rows_k, :])
+        sums_x[rows_k, :] = sums_x[rows_k, :] + jnp.where(there, face, 0.0)
+    for k, (rows_k, there) in enumerate(ends_y):
+        near_end = 7 - 7 * k
+        mine = adv_q[1, rows_k, :] - side_line(three, k, 1)
+        line = side_line(three, k, 3) + (0.5 * slope[near_end][near_end]) * mine
+        line = line * (thick * inverse_q[rows_k, :])
+        sums_y[rows_k, :] = sums_y[rows_k, :] + jnp.where(there, line, 0.0)
+    receive([ops_q.at[0], mass_q], ones[0], later)
     hear(1)
     vouch(2)
-    for c in range(3):
-        adv_ref[c] = adv[c].reshape(8, 16, 128)
-    receive([ops_q.at[0], mass_q], ones[0], copies)
-    hear(2)
+    z0 = 0.05 * (scale_x * sums_x[...] + scale_y * sums_y[...] + scale_z * along) - ops_q[0]
 
     def dot(first, second, scale):
         return jnp.sum(first * second * scale, axis=0, keepdims=True)
 
-    z0 = ops_q[0]
     image = operate(z0)
     ops_q[1] = image
     pack(ops_q.at[1], ones[1], 0)
-    sx, sy, sc = ones[1][:3]
     lines_q[...] = jnp.sum((image * plain_ref[7]).reshape(16, 8, 128), axis=1)
     for k, end in ((0, 7), (1, 0)):
         face = stiff[end][0] * image[0:16]
         for i in range(1, 8):
             face = face + stiff[end][i] * image[16 * i : 16 * i + 16]
-        sx[k, 1] = face
-        sc[2 * k, 2:3, :] = face[15:16]
-        sc[2 * k + 1, 2:3, :] = face[0:1]
-        line = lines_q[pl.ds(1 - k, 8, stride=2), :]
-        sy[k, 1] = line
-        sc[k, 1:2, :] = line[7:8]
-        sc[2 + k, 1:2, :] = line[0:1]
-    copies = launch(ones[1], 2, 2, far=True)
+        attach(ones[1], 1, k, face)
+    copies = launch(ones[1], 2, 2, far=1)
     flights += copies
+    hear(2)
     vouch(3)
+    for c in range(3):
+        adv_ref[c] = adv[c].reshape(8, 16, 128)
     part[0, 0:1, :] = dot(z0, z0, inverse_mult)
     part[0, 6:8, :] = jnp.zeros((2, 128), jnp.float32)
     receive([ops_q.at[1]], ones[1], copies)
@@ -518,10 +558,9 @@
     along = mul(joined(z1), right_ref[op_z, :])
     sums_x[...] = apart[:128]
     sums_y[...] = apart[128:]
-    two = (me_x > 1, me_x < count_x - 2)
     for k, (rows_k, there) in enumerate(ends_x):
         mine = ops_q[1, rows_k, :] - side_face(rx[k, 0], rc, k, 0)
-        other = jnp.where(two[k], side_face(far_x[k], far_c, k, 0), 0.0)
+        other = jnp.where(two[k], side_face(far_x[1, k], far_c[1], k, 0), 0.0)
         face = side_face(rx[k, 1], rc, k, 2) + stiff[7][7] * mine + stiff[7][0] * other
         sums_x[rows_k, :] = sums_x[rows_k, :] + jnp.where(there, face, 0.0)
     for k, (rows_k, there) in enumerate(ends_y):
@@ -632,11 +671,11 @@
             dma((7,)),
             vmem((3, 128, 128), f32),
             vmem((4, 128, 128), f32),
-            vmem((2, 3, 16, 128), f32),
-            vmem((2, 3, 8, 128), f32),
+            vmem((2, 4, 16, 128), f32),
+            vmem((2, 4, 8, 128), f32),
             vmem((4, 8, 128), f32),
-            vmem((2, 3, 16, 128), f32),
-            vmem((2, 3, 8, 128), f32),
+            vmem((2, 4, 16, 128), f32),
+            vmem((2, 4, 8, 128), f32),
             vmem((4, 8, 128), f32),
             vmem((3, 2, 2, 16, 128), f32),
             vmem((3, 2, 2, 8, 128), f32),
@@ -656,8 +695,9 @@
             vmem((16, 128), f32),
             vmem((128, 128), f32),
             vmem((128, 128), f32),
-            vmem((2, 16, 128), f32),
-            vmem((4, 8, 128), f32),
+            vmem((2, 2, 16, 128), f32),
+            vmem((2, 4, 8, 128), f32),
+            vmem((128, 128), f32),
         ],
         compiler_params=pltpu.CompilerParams(
             collective_id=0, has_side_effects=True, vmem_limit_bytes=54700 * 1024

time: 49.5 us -> 46.5 us (0.939)
  Pallas kernels: 47.8 us -> 44.8 us
    pallas_call x1, Pallas kernels: 47.1 us -> 44.1 us  [per_device(): pl.pallas_call(functools.partial(kernel, sizes), out_shape=(shape_of(velo...]
where the time goes in v6:
time: 46.5 us; the launch traced here: 46.3 us
  Pallas kernels  44.8 us (96%)
  local copies, waits for them, and re-layouts  0.83 us (2%)
  between operations  0.65 us (1%)
    pallas_call x1, Pallas kernels, per_device(): pl.pallas_call(functools.partial(kernel, sizes), out_shape=(shape_of(velo...  44.1 us

profile of v6, /device:TPU:1, one launch (start us, length us, event | category | flops | bytes accessed | tf_op | source)
XLA Modules:
  0.0 46.3 jit_solution(13618971156208818366)
XLA Ops:
  0.6 0.0 copy-start
  0.6 0.8 %copy-done = f32[8,16,128]{2,1,0:T(8,128)S(1)} copy-done((f32[8,16,128]{2,1,0:T(8,128)S(1)}, f32[8,16,128]{2,1,0:T(8,128)}, u32[]{:S(2)}) %copy-start) | copy-done | bytes 65560
  1.5 44.1 %shard_map.94 = (f32[3,8,16,128]{3,2,1,0:T(8,128)S(1)}, f32[8,16,128]{2,1,0:T(8,128)S(1)}, f32[8,16,128]{2,1,0:T(8,128)S(1)}) custom-call(f32[3,8,16,128]{3,2,1,0:T(8,128)} %vel_hbm.1, f32[8,16,128]{2,1,0:T(8,128)S(1)} %copy-done, bf16[384,512]{1,0:T(8,128)(2,1)} %constant.10.clone.fine_z_hbm, bf16[496,432]{1,0:T(8,128)(2,1)} %constant.11.clone.fine_xy_hbm, ...), custom_call_target="tpu_custom_call" | custom-call | tf_op jit(solution)/shard_map/pallas_call | solution.py:660
  45.5 0.7 %shard_map.95 = (f32[3,8,16,128]{3,2,1,0:T(8,128)}, f32[8,16,128]{2,1,0:T(8,128)}, f32[8,16,128]{2,1,0:T(8,128)}) custom-call(f32[3,8,16,128]{3,2,1,0:T(8,128)S(1)} %get-tuple-element.6.refs_0_, f32[8,16,128]{2,1,0:T(8,128)S(1)} %get-tuple-element.7.refs_1_, f32[8,16,128]{2,1,0:T(8,128)S(1)} %get-tuple-element.8.refs_2_), custom_call_target="tpu_custom_call" | custom-call | tf_op jit(solution)/shard_map/pallas_call | solution.py:706
Async XLA Ops:
  0.6 0.8 %copy-start = (f32[8,16,128]{2,1,0:T(8,128)S(1)}, f32[8,16,128]{2,1,0:T(8,128)}, u32[]{:S(2)}) copy-start(f32[8,16,128]{2,1,0:T(8,128)} %rea_hbm.1) | copy-start | bytes 196612

commit v7 on v6

--- a/solution.py
+++ b/solution.py
@@ -298,7 +298,7 @@
         [by_z(2), by_z(-2)] + near[4:],
         near[4:] + [(me_x, me_pair * 2 + 1 - me_core)],
     )
-    partners = [at_side(side) for side in SIDES + FAR] + near
+    partners = [at_side(side) for side in FAR + SIDES] + near
 
     barrier = pltpu.get_barrier_semaphore()
     for who in partners:
@@ -389,11 +389,12 @@
         sx, sy, sc, rx, ry, rc = bufs
         used = pl.ds(0, comps)
         moves = []
+        if far is not None:
+            for k in range(4):
+                moves.append((FAR[2 + k], sc.at[k], far_c.at[far, k]))
         for k in range(4):
             moves.append((SIDES[4 + k], sc.at[k], rc.at[k]))
         if far is not None:
-            for k in range(4):
-                moves.append((FAR[2 + k], sc.at[k], far_c.at[far, k]))
             for k in range(2):
                 moves.append((FAR[k], sx.at[k, 0], far_x.at[far, k]))
         for k in range(2):

time: 46.5 us -> 46.3 us (level)
  no operation moved by 1% of the time
where the time goes in v7:
time: 46.3 us; the launch traced here: 46.1 us
  Pallas kernels  44.6 us (96%)
  local copies, waits for them, and re-layouts  0.83 us (2%)
  between operations  0.65 us (1%)
    pallas_call x1, Pallas kernels, per_device(): pl.pallas_call(functools.partial(kernel, sizes), out_shape=(shape_of(velo...  43.9 us

profile of v7, /device:TPU:1, one launch (start us, length us, event | category | flops | bytes accessed | tf_op | source)
XLA Modules:
  0.0 46.1 jit_solution(12870129120757660209)
XLA Ops:
  0.6 0.0 copy-start
  0.6 0.8 %copy-done = f32[8,16,128]{2,1,0:T(8,128)S(1)} copy-done((f32[8,16,128]{2,1,0:T(8,128)S(1)}, f32[8,16,128]{2,1,0:T(8,128)}, u32[]{:S(2)}) %copy-start) | copy-done | bytes 65560
  1.5 43.9 %shard_map.94 = (f32[3,8,16,128]{3,2,1,0:T(8,128)S(1)}, f32[8,16,128]{2,1,0:T(8,128)S(1)}, f32[8,16,128]{2,1,0:T(8,128)S(1)}) custom-call(f32[3,8,16,128]{3,2,1,0:T(8,128)} %vel_hbm.1, f32[8,16,128]{2,1,0:T(8,128)S(1)} %copy-done, bf16[384,512]{1,0:T(8,128)(2,1)} %constant.10.clone.fine_z_hbm, bf16[496,432]{1,0:T(8,128)(2,1)} %constant.11.clone.fine_xy_hbm, ...), custom_call_target="tpu_custom_call" | custom-call | tf_op jit(solution)/shard_map/pallas_call | solution.py:661
  45.3 0.7 %shard_map.95 = (f32[3,8,16,128]{3,2,1,0:T(8,128)}, f32[8,16,128]{2,1,0:T(8,128)}, f32[8,16,128]{2,1,0:T(8,128)}) custom-call(f32[3,8,16,128]{3,2,1,0:T(8,128)S(1)} %get-tuple-element.6.refs_0_, f32[8,16,128]{2,1,0:T(8,128)S(1)} %get-tuple-element.7.refs_1_, f32[8,16,128]{2,1,0:T(8,128)S(1)} %get-tuple-element.8.refs_2_), custom_call_target="tpu_custom_call" | custom-call | tf_op jit(solution)/shard_map/pallas_call | solution.py:707
Async XLA Ops:
  0.6 0.8 %copy-start = (f32[8,16,128]{2,1,0:T(8,128)S(1)}, f32[8,16,128]{2,1,0:T(8,128)}, u32[]{:S(2)}) copy-start(f32[8,16,128]{2,1,0:T(8,128)} %rea_hbm.1) | copy-start | bytes 196612

commit v8 on v7

--- a/solution.py
+++ b/solution.py
@@ -544,7 +544,9 @@
             face = face + stiff[end][i] * image[16 * i : 16 * i + 16]
         attach(ones[1], 1, k, face)
     copies = launch(ones[1], 2, 2, far=1)
-    flights += copies
+    for copy in flights:
+        copy.wait_send()
+    flights = list(copies)
     hear(2)
     vouch(3)
     for c in range(3):
@@ -597,7 +599,9 @@
             ops_q[3] = last
             pack(ops_q.at[3], ones[2], 0)
             copies = launch(ones[2], 3, 1)
-            flights += copies
+        for copy in flights:
+            copy.wait_send()
+        flights = copies_in
         for copy in copies_in:
             copy.wait_recv()
         total = part[index]
@@ -605,9 +609,9 @@
             total = total + got[slot + k]
         if index < 1:
             part[index + 1] = total
-        flights += copies_in
         slot += len(stage)
 
+    flights = flights + copies
     receive([ops_q.at[3]], ones[2], copies)
     sums = jnp.broadcast_to(jnp.sum(total, axis=1, keepdims=True), (8, 128))
     g00, g01, g11, g12, g22, g23 = (sums[k : k + 1, :] for k in range(6))

time: 46.3 us -> 46.2 us (level)
  no operation moved by 1% of the time
where the time goes in v8:
time: 46.2 us; the launch traced here: 46 us
  Pallas kernels  44.5 us (96%)
  local copies, waits for them, and re-layouts  0.83 us (2%)
  between operations  0.65 us (1%)
    pallas_call x1, Pallas kernels, per_device(): pl.pallas_call(functools.partial(kernel, sizes), out_shape=(shape_of(velo...  43.8 us

profile of v8, /device:TPU:1, one launch (start us, length us, event | category | flops | bytes accessed | tf_op | source)
XLA Modules:
  0.0 46.0 jit_solution(2238861439691225436)
XLA Ops:
  0.6 0.0 copy-start
  0.6 0.8 %copy-done = f32[8,16,128]{2,1,0:T(8,128)S(1)} copy-done((f32[8,16,128]{2,1,0:T(8,128)S(1)}, f32[8,16,128]{2,1,0:T(8,128)}, u32[]{:S(2)}) %copy-start) | copy-done | bytes 65560
  1.5 43.8 %shard_map.94 = (f32[3,8,16,128]{3,2,1,0:T(8,128)S(1)}, f32[8,16,128]{2,1,0:T(8,128)S(1)}, f32[8,16,128]{2,1,0:T(8,128)S(1)}) custom-call(f32[3,8,16,128]{3,2,1,0:T(8,128)} %vel_hbm.1, f32[8,16,128]{2,1,0:T(8,128)S(1)} %copy-done, bf16[384,512]{1,0:T(8,128)(2,1)} %constant.10.clone.fine_z_hbm, bf16[496,432]{1,0:T(8,128)(2,1)} %constant.11.clone.fine_xy_hbm, ...), custom_call_target="tpu_custom_call" | custom-call | tf_op jit(solution)/shard_map/pallas_call | solution.py:665
  45.3 0.7 %shard_map.95 = (f32[3,8,16,128]{3,2,1,0:T(8,128)}, f32[8,16,128]{2,1,0:T(8,128)}, f32[8,16,128]{2,1,0:T(8,128)}) custom-call(f32[3,8,16,128]{3,2,1,0:T(8,128)S(1)} %get-tuple-element.6.refs_0_, f32[8,16,128]{2,1,0:T(8,128)S(1)} %get-tuple-element.7.refs_1_, f32[8,16,128]{2,1,0:T(8,128)S(1)} %get-tuple-element.8.refs_2_), custom_call_target="tpu_custom_call" | custom-call | tf_op jit(solution)/shard_map/pallas_call | solution.py:711
Async XLA Ops:
  0.6 0.8 %copy-start = (f32[8,16,128]{2,1,0:T(8,128)S(1)}, f32[8,16,128]{2,1,0:T(8,128)}, u32[]{:S(2)}) copy-start(f32[8,16,128]{2,1,0:T(8,128)} %rea_hbm.1) | copy-start | bytes 196612

commit v9 on v7

--- a/solution.py
+++ b/solution.py
@@ -269,19 +269,6 @@
         steps = [(i, j) for i in range(count_a) for j in range(count_b) if (i, j) != (0, 0)]
         return sorted(steps, key=lambda s: -hops(s[0], count_a) - hops(s[1], count_b))
 
-    stages = (
-        [
-            (me_high * low_count + turn(me_low, i, low_count), me_pair * 2 + turn(me_core, j, 2))
-            for i, j in far_first(low_count, 2)
-        ],
-        [
-            (
-                turn(me_high, i, high_count) * low_count + me_low,
-                turn(me_pair, j, count_y // 2) * 2 + me_core,
-            )
-            for i, j in far_first(high_count, count_y // 2)
-        ],
-    )
     def by_z(step):
         return me_high * low_count + turn(me_low, step, low_count), me_y
 
@@ -544,6 +531,19 @@
             face = face + stiff[end][i] * image[16 * i : 16 * i + 16]
         attach(ones[1], 1, k, face)
     copies = launch(ones[1], 2, 2, far=1)
+    stages = (
+        [
+            (me_high * low_count + turn(me_low, i, low_count), me_pair * 2 + turn(me_core, j, 2))
+            for i, j in far_first(low_count, 2)
+        ],
+        [
+            (
+                turn(me_high, i, high_count) * low_count + me_low,
+                turn(me_pair, j, count_y // 2) * 2 + me_core,
+            )
+            for i, j in far_first(high_count, count_y // 2)
+        ],
+    )
     flights += copies
     hear(2)
     vouch(3)

time: 46.3 us -> 46.3 us (level)
  no operation moved by 1% of the time
where the time goes in v9:
time: 46.3 us; the launch traced here: 46.1 us
  Pallas kernels  44.6 us (96%)
  local copies, waits for them, and re-layouts  0.83 us (2%)
  between operations  0.65 us (1%)
    pallas_call x1, Pallas kernels, per_device(): pl.pallas_call(functools.partial(kernel, sizes), out_shape=(shape_of(velo...  43.8 us

profile of v9, /device:TPU:1, one launch (start us, length us, event | category | flops | bytes accessed | tf_op | source)
XLA Modules:
  0.0 46.1 jit_solution(5940253658594698478)
XLA Ops:
  0.6 0.0 copy-start
  0.6 0.8 %copy-done = f32[8,16,128]{2,1,0:T(8,128)S(1)} copy-done((f32[8,16,128]{2,1,0:T(8,128)S(1)}, f32[8,16,128]{2,1,0:T(8,128)}, u32[]{:S(2)}) %copy-start) | copy-done | bytes 65560
  1.5 43.8 %shard_map.94 = (f32[3,8,16,128]{3,2,1,0:T(8,128)S(1)}, f32[8,16,128]{2,1,0:T(8,128)S(1)}, f32[8,16,128]{2,1,0:T(8,128)S(1)}) custom-call(f32[3,8,16,128]{3,2,1,0:T(8,128)} %vel_hbm.1, f32[8,16,128]{2,1,0:T(8,128)S(1)} %copy-done, bf16[384,512]{1,0:T(8,128)(2,1)} %constant.10.clone.fine_z_hbm, bf16[496,432]{1,0:T(8,128)(2,1)} %constant.11.clone.fine_xy_hbm, ...), custom_call_target="tpu_custom_call" | custom-call | tf_op jit(solution)/shard_map/pallas_call | solution.py:661
  45.3 0.7 %shard_map.95 = (f32[3,8,16,128]{3,2,1,0:T(8,128)}, f32[8,16,128]{2,1,0:T(8,128)}, f32[8,16,128]{2,1,0:T(8,128)}) custom-call(f32[3,8,16,128]{3,2,1,0:T(8,128)S(1)} %get-tuple-element.6.refs_0_, f32[8,16,128]{2,1,0:T(8,128)S(1)} %get-tuple-element.7.refs_1_, f32[8,16,128]{2,1,0:T(8,128)S(1)} %get-tuple-element.8.refs_2_), custom_call_target="tpu_custom_call" | custom-call | tf_op jit(solution)/shard_map/pallas_call | solution.py:707
Async XLA Ops:
  0.6 0.8 %copy-start = (f32[8,16,128]{2,1,0:T(8,128)S(1)}, f32[8,16,128]{2,1,0:T(8,128)}, u32[]{:S(2)}) copy-start(f32[8,16,128]{2,1,0:T(8,128)} %rea_hbm.1) | copy-start | bytes 196612
